TPU v7x, 32 devices: a whole 2x2x4 slice. The times are simulated.
32 devices in a mesh: grp: 2 (over y), ta: 4 (over z), ha: 4 (over x, core).
Axes of the slice: x: 2, y: 2, z: 4, core: 2. Of those that a mesh axis runs over, the one named last changes fastest.
Arguments:
- queries: bfloat16 [48, 16, 8, 1536], P(('grp', 'ta'), 'ha'), parts along dimension 0, may hold values from -6 to 6
- key_rows: bfloat16 [48, 16, 8, 1536], P(('grp', 'ta'), 'ha'), parts along dimension 0, may hold values from -6 to 6
- value_rows: bfloat16 [48, 16, 8, 1536], P(('grp', 'ta'), 'ha'), parts along dimension 0, may hold values from -6 to 6
- out_grad: bfloat16 [48, 16, 8, 1536], P(('grp', 'ta'), 'ha'), parts along dimension 0, may hold values from -192 to 192
- logsumexp: float32 [48, 16, 8, 12], P(('grp', 'ta'), 'ha'), parts along dimension 0, may hold values from 6.5 to 8.5
- out_dot: float32 [48, 16, 8, 12], P(('grp', 'ta'), 'ha'), parts along dimension 0, may hold values from -384 to 384
- text_keys: bfloat16 [256, 1536], P(('grp', 'ta')), parts along dimension 0, may hold values from -6 to 6
- text_values: bfloat16 [256, 1536], P(('grp', 'ta')), parts along dimension 0, may hold values from -6 to 6
- text_length: int32 [2], P('grp'), parts along dimension 0, may hold values from 16 to 128
- window_reach: int32 [12, 2], replicated, may hold values from 0 to 1
Outputs:
- query_grad: bfloat16 [48, 16, 8, 1536], P(('grp', 'ta'), 'ha'), parts along dimension 0
- key_grad: bfloat16 [48, 16, 8, 1536], P(('grp', 'ta'), 'ha'), parts along dimension 0
- value_grad: bfloat16 [48, 16, 8, 1536], P(('grp', 'ta'), 'ha'), parts along dimension 0
- text_key_grad: bfloat16 [256, 1536], P(('grp', 'ta')), parts along dimension 0
- text_value_grad: bfloat16 [256, 1536], P(('grp', 'ta')), parts along dimension 0
There are 2 independent parts, one for each index of `grp`. A program takes and returns all parts, laid end to end along the dimension named above; an argument that names none is the same for every part. Nothing has to cross between parts.
All inputs are finite; a program needn't handle non-finite values.
Results may differ from a plain program's by a relative error of at most 0.0059.
Values may be sent and summed in bfloat16 or wider, within the bound.
A program may use at most 128 MiB of HBM per device.

v0:
```python
import jax
import jax.numpy as jnp
from jax import lax
from jax.sharding import PartitionSpec as P

TILE_W = 8


def from_partner(block, axis, bit):
    count = lax.axis_size(axis)
    route = []
    for low in range(count):
        high = low | 1 << bit
        if high != low and high < count:
            route += [(low, high), (high, low)]
    return lax.ppermute(block, axis, route)


def padded(block, sides, width):
    for axis, dim in sides:
        count = lax.axis_size(axis)
        forward = [(i, i + 1) for i in range(count - 1)]
        backward = [(target, source) for source, target in forward]
        low = lax.ppermute(
            lax.slice_in_dim(block, block.shape[dim] - width, None, axis=dim), axis, forward
        )
        high = lax.ppermute(lax.slice_in_dim(block, 0, width, axis=dim), axis, backward)
        block = jnp.concatenate([low, block, high], axis=dim)
    return block


def passed_along(block, axis, distance):
    devices = range(lax.axis_size(axis))
    route = [(i - distance, i) for i in devices if i - distance in devices]
    return lax.ppermute(block, axis, route)


def rounded(values):
    return lax.optimization_barrier(values.astype(jnp.bfloat16)).astype(jnp.float32)


def column(array, head_index, head_size):
    return lax.dynamic_slice_in_dim(array, head_index * head_size, head_size, array.ndim - 1)


def stat_column(array, head_index):
    return lax.dynamic_index_in_dim(array, head_index, array.ndim - 1, False)


def put_column(array, piece, head_index, head_size):
    return lax.dynamic_update_slice_in_dim(
        array, piece.astype(array.dtype), head_index * head_size, array.ndim - 1
    )


def stack_halves(own_part, twin_part, half_index):
    lower_half = jnp.where(half_index == 0, own_part, twin_part)
    upper_half = jnp.where(half_index == 0, twin_part, own_part)
    return jnp.concatenate([lower_half, upper_half], axis=1)


def split_halves(summed, half_index, band_rows):
    lower_half = summed[:, :band_rows]
    upper_half = summed[:, band_rows:]
    return (
        jnp.where(half_index == 0, lower_half, upper_half),
        jnp.where(half_index == 0, upper_half, lower_half),
    )


def pair_grads(
    query_set,
    grad_set,
    logsum_set,
    dot_set,
    key_set,
    value_set,
    allowed,
    scaling,
    band_rows,
    width_tiles,
):
    query_tiles = query_set.shape[0]
    frames = query_set.shape[1]
    query_band = query_set.shape[2]
    width_cols = query_set.shape[3]
    head_size = query_set.shape[4]
    key_tiles = key_set.shape[0]
    key_band = key_set.shape[2]
    tile_cols = width_cols // width_tiles
    query_shape = (
        query_tiles,
        frames,
        query_band // band_rows,
        band_rows,
        width_tiles,
        tile_cols,
        head_size,
    )
    key_shape = (
        key_tiles,
        frames,
        key_band // band_rows,
        band_rows,
        width_tiles,
        tile_cols,
        head_size,
    )
    stat_shape = (query_tiles, frames, query_band // band_rows, band_rows, width_tiles, tile_cols)
    query_grid = query_set.reshape(query_shape)
    grad_grid = grad_set.reshape(query_shape)
    key_grid = key_set.reshape(key_shape)
    value_grid = value_set.reshape(key_shape)
    logsum_grid = logsum_set.reshape(stat_shape).transpose(4, 0, 1, 2, 3, 5)[
        ..., None, None, None, None, None
    ]
    dot_grid = dot_set.reshape(stat_shape).transpose(4, 0, 1, 2, 3, 5)[
        ..., None, None, None, None, None
    ]
    pattern = "atgywxd,buhzwvd->watgyxbuhzv"
    scores = jnp.einsum(pattern, query_grid, key_grid, preferred_element_type=jnp.float32)
    visible = allowed[None, :, None, None, None, None, :, None, None, None, None]
    weight = jnp.where(visible, jnp.exp(scores * scaling - logsum_grid), 0.0)
    prob_data = weight.astype(jnp.bfloat16)
    prob_grad = jnp.einsum(pattern, grad_grid, value_grid, preferred_element_type=jnp.float32)
    score_grad = (weight * (prob_grad - dot_grid) * scaling).astype(jnp.bfloat16)
    query_terms = jnp.einsum(
        "watgyxbuhzv,buhzwvd->atgywxbhd", score_grad, key_grid, preferred_element_type=jnp.float32
    )
    key_terms = jnp.einsum(
        "watgyxbuhzv,atgywxd->buhzwvagd", score_grad, query_grid, preferred_element_type=jnp.float32
    )
    value_terms = jnp.einsum(
        "watgyxbuhzv,atgywxd->buhzwvagd", prob_data, grad_grid, preferred_element_type=jnp.float32
    )
    query_part = jnp.sum(rounded(query_terms), axis=(6, 7)).reshape(
        query_tiles, frames, query_band, width_cols, head_size
    )
    key_part = jnp.sum(rounded(key_terms), axis=(6, 7)).reshape(
        key_tiles, frames, key_band, width_cols, head_size
    )
    value_part = jnp.sum(rounded(value_terms), axis=(6, 7)).reshape(
        key_tiles, frames, key_band, width_cols, head_size
    )
    return (query_part, key_part, value_part)


def text_grads(
    query_part,
    grad_part,
    logsum_part,
    dot_part,
    text_key_part,
    text_value_part,
    text_ok,
    scaling,
    width_tiles,
):
    frames = query_part.shape[0]
    band_rows = query_part.shape[1]
    width_cols = query_part.shape[2]
    head_size = query_part.shape[3]
    tile_cols = width_cols // width_tiles
    query_grid = query_part.reshape(frames, band_rows, width_tiles, tile_cols, head_size)
    grad_grid = grad_part.reshape(frames, band_rows, width_tiles, tile_cols, head_size)
    logsum_grid = logsum_part.reshape(frames, band_rows, width_tiles, tile_cols).transpose(
        2, 0, 1, 3
    )[..., None]
    dot_grid = dot_part.reshape(frames, band_rows, width_tiles, tile_cols).transpose(2, 0, 1, 3)[
        ..., None
    ]
    scores = jnp.einsum(
        "tywxd,jd->wtyxj", query_grid, text_key_part, preferred_element_type=jnp.float32
    )
    weight = jnp.where(text_ok, jnp.exp(scores * scaling - logsum_grid), 0.0)
    prob_data = weight.astype(jnp.bfloat16)
    prob_grad = jnp.einsum(
        "tywxd,jd->wtyxj", grad_grid, text_value_part, preferred_element_type=jnp.float32
    )
    score_grad = (weight * (prob_grad - dot_grid) * scaling).astype(jnp.bfloat16)
    text_query = jnp.einsum(
        "wtyxj,jd->tywxd", score_grad, text_key_part, preferred_element_type=jnp.float32
    ).reshape(frames, band_rows, width_cols, head_size)
    text_key = jnp.einsum(
        "wtyxj,tywxd->jd", score_grad, query_grid, preferred_element_type=jnp.float32
    )
    text_value = jnp.einsum(
        "wtyxj,tywxd->jd", prob_data, grad_grid, preferred_element_type=jnp.float32
    )
    return (text_query, text_key, text_value)


def per_device(
    queries,
    key_rows,
    value_rows,
    out_grad,
    logsumexp,
    out_dot,
    text_keys,
    text_values,
    text_length,
    window_reach,
):
    frames = queries.shape[0]
    band_rows = queries.shape[1]
    width_cols = queries.shape[2]
    hidden = queries.shape[3]
    head_count = logsumexp.shape[3]
    head_size = hidden // head_count
    width_tiles = width_cols // TILE_W
    scaling = head_size ** (-0.5)
    half_index = lax.axis_index("ha") % 2
    time_tile = lax.axis_index("ta")
    tile_count = lax.axis_size("ta")
    gathered = (
        lax.all_gather(text_keys, "ta", axis=0, tiled=True),
        lax.all_gather(text_values, "ta", axis=0, tiled=True),
    )
    text_count = gathered[0].shape[0]
    text_ok = lax.iota(jnp.int32, text_count) < text_length[0]
    offsets = lax.iota(jnp.int32, 3) - 1
    tile_ok = jnp.stack([time_tile > 0, time_tile >= 0, time_tile < tile_count - 1])
    text_zero = jnp.zeros((text_count, hidden), jnp.float32)
    shape_ext = (3, frames, 2 * band_rows, width_cols, hidden)
    twin_rows = from_partner((key_rows, value_rows), "ha", 0)
    key_tile = stack_halves(key_rows, twin_rows[0], half_index)
    value_tile = stack_halves(value_rows, twin_rows[1], half_index)
    beside_all = (padded(key_tile, (("ta", 0),), frames), padded(value_tile, (("ta", 0),), frames))
    key_ext = beside_all[0].reshape(shape_ext)
    value_ext = beside_all[1].reshape(shape_ext)

    def head_step(head_index, carried):
        query_out, key_out, value_out, key_text_sum, value_text_sum = carried
        allowed = (
            tile_ok
            & (offsets >= -window_reach[head_index, 0])
            & (offsets <= window_reach[head_index, 1])
        )[None, :]
        query_part = column(queries, head_index, head_size)
        grad_part = column(out_grad, head_index, head_size)
        logsum_part = stat_column(logsumexp, head_index)
        dot_part = stat_column(out_dot, head_index)
        query_terms, key_terms, value_terms = pair_grads(
            query_part[None],
            grad_part[None],
            logsum_part[None],
            dot_part[None],
            column(key_ext, head_index, head_size),
            column(value_ext, head_index, head_size),
            allowed,
            scaling,
            band_rows,
            width_tiles,
        )
        text_query, text_key, text_value = text_grads(
            query_part,
            grad_part,
            logsum_part,
            dot_part,
            column(gathered[0], head_index, head_size),
            column(gathered[1], head_index, head_size),
            text_ok,
            scaling,
            width_tiles,
        )
        query_out = put_column(query_out, query_terms[0] + text_query, head_index, head_size)
        key_out = put_column(key_out, key_terms, head_index, head_size)
        value_out = put_column(value_out, value_terms, head_index, head_size)
        key_text_sum = put_column(key_text_sum, text_key, head_index, head_size)
        value_text_sum = put_column(value_text_sum, text_value, head_index, head_size)
        return (query_out, key_out, value_out, key_text_sum, value_text_sum)

    initial = (
        jnp.zeros_like(queries),
        jnp.zeros(shape_ext, jnp.bfloat16),
        jnp.zeros(shape_ext, jnp.bfloat16),
        text_zero,
        text_zero,
    )
    query_grad, key_ext_grad, value_ext_grad, key_text_sum, value_text_sum = lax.fori_loop(
        0, head_count, head_step, initial
    )
    own_key = key_ext_grad[1].astype(jnp.float32)
    own_value = value_ext_grad[1].astype(jnp.float32)
    for shift_by, slot_index in ((-1, 0), (1, 2)):
        arrived = passed_along(
            (key_ext_grad[slot_index], value_ext_grad[slot_index]), "ta", shift_by
        )
        own_key = own_key + arrived[0].astype(jnp.float32)
        own_value = own_value + arrived[1].astype(jnp.float32)
    mine_key, other_key = split_halves(own_key, half_index, band_rows)
    mine_value, other_value = split_halves(own_value, half_index, band_rows)
    returned = from_partner((other_key, other_value), "ha", 0)
    key_grad = (mine_key + returned[0]).astype(jnp.bfloat16)
    value_grad = (mine_value + returned[1]).astype(jnp.bfloat16)
    text_sums = (
        lax.psum_scatter(key_text_sum, "ta", scatter_dimension=0, tiled=True),
        lax.psum_scatter(value_text_sum, "ta", scatter_dimension=0, tiled=True),
    )
    text_totals = lax.psum((text_sums[0], text_sums[1]), "ha")
    return (
        query_grad,
        key_grad,
        value_grad,
        text_totals[0].astype(jnp.bfloat16),
        text_totals[1].astype(jnp.bfloat16),
    )


def solution(mesh):
    in_specs = (
        P(("grp", "ta"), "ha", None, None),
        P(("grp", "ta"), "ha", None, None),
        P(("grp", "ta"), "ha", None, None),
        P(("grp", "ta"), "ha", None, None),
        P(("grp", "ta"), "ha", None, None),
        P(("grp", "ta"), "ha", None, None),
        P(("grp", "ta"), None),
        P(("grp", "ta"), None),
        P("grp"),
        P(),
    )
    out_specs = (
        P(("grp", "ta"), "ha", None, None),
        P(("grp", "ta"), "ha", None, None),
        P(("grp", "ta"), "ha", None, None),
        P(("grp", "ta"), None),
        P(("grp", "ta"), None),
    )
    return jax.shard_map(
        per_device, mesh=mesh, in_specs=in_specs, out_specs=out_specs, check_vma=False
    )
```

profile of v0, /device:TPU:0, one launch (start us, length us, event | category | flops | bytes accessed | tf_op | source)
XLA Modules:
  0.0 578.8 jit_solution(3529728020838082925)
XLA Ops:
  14.3 6.5 %collective-permute-start.1 = (bf16[6,8,8,1536]{3,2,1,0:T(8,128)(2,1)}, bf16[6,8,8,1536]{3,2,1,0:T(8,128)(2,1)}, u32[]{:S(2)}, u32[]{:S(2)}) collective-permute-start(bf16[6,8,8,1536]{3,2,1,0:T(8,128)(2,1)} %pad_maximum_fusion.2), channel_id=1, source_target_pairs={{0,4},{4,8},{8,12},{1,5},{5,9},{9,13},{2,6},{6,10},{10,14},{3,7},{... | collective-permute-start | bytes 3538952 | tf_op jit(solution)/shard_map/ppermute | solution.py:24
  23.2 5.6 collective-permute-start.4
  32.4 51.9 %all_gather.6 = bf16[128,1536]{1,0:T(8,128)(2,1)} all-gather(bf16[32,1536]{1,0:T(8,128)(2,1)} %param.18), channel_id=1, replica_groups=mesh['grp'=2,'ta'=4,'ha'=4] {'ta'}, dimensions={0}, use_global_device_ids=true | all-gather | bytes 491520 | tf_op jit(solution)/shard_map/all_gather | solution.py:217
  84.3 17.4 %all_gather.7 = bf16[128,1536]{1,0:T(8,128)(2,1)} all-gather(bf16[32,1536]{1,0:T(8,128)(2,1)} %param.19), channel_id=1, replica_groups=mesh['grp'=2,'ta'=4,'ha'=4] {'ta'}, dimensions={0}, use_global_device_ids=true | all-gather | bytes 491520 | tf_op jit(solution)/shard_map/all_gather | solution.py:218
  113.5 355.2 %while.23 = (s32[]{:T(128)}, bf16[6,4,8,1536]{3,2,1,0:T(8,128)(2,1)}, bf16[3,6,8,8,1536]{4,3,2,1,0:T(8,128)(2,1)S(1)}, bf16[3,6,8,8,1536]{4,3,2,1,0:T(8,128)(2,1...) while((s32[]{:T(128)}, ...), condition=%wide.region_2.3_spmd.clone.clone, body=%wide.region_0.2_spmd.clone.clone.sunk | while | flops 317964416 | bytes 9728327 | solution.py:281
  120.2 5.9 %multiply_convert_fusion.2 = bf16[6,4,8,3,6,2,4,8]{7,2,6,5,4,3,1,0:T(8,128)(2,1)S(1)} fusion(f32[6,4,8,3,6,2,4,8]{7,2,6,5,4,3,1,0:T(8,128)S(1)} %fusion.133, bf16[3,6,2,4,8,128,1,1]{5,4,3,2,1,0,7,6:T(8,128)(2,1)S(1)} %bitcast.242, f32[6,4,8]{2,1,0:T(4,128)S(1)} %get-tuple-element.564, f32[6,4,8]{2,1,0:T(4,128)S(1)} %get-tuple-element.565, ...), kind=kOutput, calls=%fused_computation.2.clone.1 | convolution fusion | flops 58171392 | bytes 1672711 | tf_op jit(solution)/shard_map/while/body/eval_jaxpr/atgywxd,buhzwvd->watgyxbuhzv/dot_general | solution.py:125
  149.7 5.9 %multiply_convert_fusion.2 = bf16[6,4,8,3,6,2,4,8]{7,2,6,5,4,3,1,0:T(8,128)(2,1)S(1)} fusion(f32[6,4,8,3,6,2,4,8]{7,2,6,5,4,3,1,0:T(8,128)S(1)} %fusion.133, bf16[3,6,2,4,8,128,1,1]{5,4,3,2,1,0,7,6:T(8,128)(2,1)S(1)} %bitcast.242, f32[6,4,8]{2,1,0:T(4,128)S(1)} %get-tuple-element.564, f32[6,4,8]{2,1,0:T(4,128)S(1)} %get-tuple-element.565, ...), kind=kOutput, calls=%fused_computation.2.clone.1 | convolution fusion | flops 58171392 | bytes 1672711 | tf_op jit(solution)/shard_map/while/body/eval_jaxpr/atgywxd,buhzwvd->watgyxbuhzv/dot_general | solution.py:125
  179.4 5.9 %multiply_convert_fusion.2 = bf16[6,4,8,3,6,2,4,8]{7,2,6,5,4,3,1,0:T(8,128)(2,1)S(1)} fusion(f32[6,4,8,3,6,2,4,8]{7,2,6,5,4,3,1,0:T(8,128)S(1)} %fusion.133, bf16[3,6,2,4,8,128,1,1]{5,4,3,2,1,0,7,6:T(8,128)(2,1)S(1)} %bitcast.242, f32[6,4,8]{2,1,0:T(4,128)S(1)} %get-tuple-element.564, f32[6,4,8]{2,1,0:T(4,128)S(1)} %get-tuple-element.565, ...), kind=kOutput, calls=%fused_computation.2.clone.1 | convolution fusion | flops 58171392 | bytes 1672711 | tf_op jit(solution)/shard_map/while/body/eval_jaxpr/atgywxd,buhzwvd->watgyxbuhzv/dot_general | solution.py:125
  209.0 5.9 %multiply_convert_fusion.2 = bf16[6,4,8,3,6,2,4,8]{7,2,6,5,4,3,1,0:T(8,128)(2,1)S(1)} fusion(f32[6,4,8,3,6,2,4,8]{7,2,6,5,4,3,1,0:T(8,128)S(1)} %fusion.133, bf16[3,6,2,4,8,128,1,1]{5,4,3,2,1,0,7,6:T(8,128)(2,1)S(1)} %bitcast.242, f32[6,4,8]{2,1,0:T(4,128)S(1)} %get-tuple-element.564, f32[6,4,8]{2,1,0:T(4,128)S(1)} %get-tuple-element.565, ...), kind=kOutput, calls=%fused_computation.2.clone.1 | convolution fusion | flops 58171392 | bytes 1672711 | tf_op jit(solution)/shard_map/while/body/eval_jaxpr/atgywxd,buhzwvd->watgyxbuhzv/dot_general | solution.py:125
  238.6 5.9 %multiply_convert_fusion.2 = bf16[6,4,8,3,6,2,4,8]{7,2,6,5,4,3,1,0:T(8,128)(2,1)S(1)} fusion(f32[6,4,8,3,6,2,4,8]{7,2,6,5,4,3,1,0:T(8,128)S(1)} %fusion.133, bf16[3,6,2,4,8,128,1,1]{5,4,3,2,1,0,7,6:T(8,128)(2,1)S(1)} %bitcast.242, f32[6,4,8]{2,1,0:T(4,128)S(1)} %get-tuple-element.564, f32[6,4,8]{2,1,0:T(4,128)S(1)} %get-tuple-element.565, ...), kind=kOutput, calls=%fused_computation.2.clone.1 | convolution fusion | flops 58171392 | bytes 1672711 | tf_op jit(solution)/shard_map/while/body/eval_jaxpr/atgywxd,buhzwvd->watgyxbuhzv/dot_general | solution.py:125
  268.2 5.9 %multiply_convert_fusion.2 = bf16[6,4,8,3,6,2,4,8]{7,2,6,5,4,3,1,0:T(8,128)(2,1)S(1)} fusion(f32[6,4,8,3,6,2,4,8]{7,2,6,5,4,3,1,0:T(8,128)S(1)} %fusion.133, bf16[3,6,2,4,8,128,1,1]{5,4,3,2,1,0,7,6:T(8,128)(2,1)S(1)} %bitcast.242, f32[6,4,8]{2,1,0:T(4,128)S(1)} %get-tuple-element.564, f32[6,4,8]{2,1,0:T(4,128)S(1)} %get-tuple-element.565, ...), kind=kOutput, calls=%fused_computation.2.clone.1 | convolution fusion | flops 58171392 | bytes 1672711 | tf_op jit(solution)/shard_map/while/body/eval_jaxpr/atgywxd,buhzwvd->watgyxbuhzv/dot_general | solution.py:125
  297.8 5.9 %multiply_convert_fusion.2 = bf16[6,4,8,3,6,2,4,8]{7,2,6,5,4,3,1,0:T(8,128)(2,1)S(1)} fusion(f32[6,4,8,3,6,2,4,8]{7,2,6,5,4,3,1,0:T(8,128)S(1)} %fusion.133, bf16[3,6,2,4,8,128,1,1]{5,4,3,2,1,0,7,6:T(8,128)(2,1)S(1)} %bitcast.242, f32[6,4,8]{2,1,0:T(4,128)S(1)} %get-tuple-element.564, f32[6,4,8]{2,1,0:T(4,128)S(1)} %get-tuple-element.565, ...), kind=kOutput, calls=%fused_computation.2.clone.1 | convolution fusion | flops 58171392 | bytes 1672711 | tf_op jit(solution)/shard_map/while/body/eval_jaxpr/atgywxd,buhzwvd->watgyxbuhzv/dot_general | solution.py:125
  327.4 5.9 %multiply_convert_fusion.2 = bf16[6,4,8,3,6,2,4,8]{7,2,6,5,4,3,1,0:T(8,128)(2,1)S(1)} fusion(f32[6,4,8,3,6,2,4,8]{7,2,6,5,4,3,1,0:T(8,128)S(1)} %fusion.133, bf16[3,6,2,4,8,128,1,1]{5,4,3,2,1,0,7,6:T(8,128)(2,1)S(1)} %bitcast.242, f32[6,4,8]{2,1,0:T(4,128)S(1)} %get-tuple-element.564, f32[6,4,8]{2,1,0:T(4,128)S(1)} %get-tuple-element.565, ...), kind=kOutput, calls=%fused_computation.2.clone.1 | convolution fusion | flops 58171392 | bytes 1672711 | tf_op jit(solution)/shard_map/while/body/eval_jaxpr/atgywxd,buhzwvd->watgyxbuhzv/dot_general | solution.py:125
  357.0 5.9 %multiply_convert_fusion.2 = bf16[6,4,8,3,6,2,4,8]{7,2,6,5,4,3,1,0:T(8,128)(2,1)S(1)} fusion(f32[6,4,8,3,6,2,4,8]{7,2,6,5,4,3,1,0:T(8,128)S(1)} %fusion.133, bf16[3,6,2,4,8,128,1,1]{5,4,3,2,1,0,7,6:T(8,128)(2,1)S(1)} %bitcast.242, f32[6,4,8]{2,1,0:T(4,128)S(1)} %get-tuple-element.564, f32[6,4,8]{2,1,0:T(4,128)S(1)} %get-tuple-element.565, ...), kind=kOutput, calls=%fused_computation.2.clone.1 | convolution fusion | flops 58171392 | bytes 1672711 | tf_op jit(solution)/shard_map/while/body/eval_jaxpr/atgywxd,buhzwvd->watgyxbuhzv/dot_general | solution.py:125
  386.6 5.9 %multiply_convert_fusion.2 = bf16[6,4,8,3,6,2,4,8]{7,2,6,5,4,3,1,0:T(8,128)(2,1)S(1)} fusion(f32[6,4,8,3,6,2,4,8]{7,2,6,5,4,3,1,0:T(8,128)S(1)} %fusion.133, bf16[3,6,2,4,8,128,1,1]{5,4,3,2,1,0,7,6:T(8,128)(2,1)S(1)} %bitcast.242, f32[6,4,8]{2,1,0:T(4,128)S(1)} %get-tuple-element.564, f32[6,4,8]{2,1,0:T(4,128)S(1)} %get-tuple-element.565, ...), kind=kOutput, calls=%fused_computation.2.clone.1 | convolution fusion | flops 58171392 | bytes 1672711 | tf_op jit(solution)/shard_map/while/body/eval_jaxpr/atgywxd,buhzwvd->watgyxbuhzv/dot_general | solution.py:125
  416.2 5.9 %multiply_convert_fusion.2 = bf16[6,4,8,3,6,2,4,8]{7,2,6,5,4,3,1,0:T(8,128)(2,1)S(1)} fusion(f32[6,4,8,3,6,2,4,8]{7,2,6,5,4,3,1,0:T(8,128)S(1)} %fusion.133, bf16[3,6,2,4,8,128,1,1]{5,4,3,2,1,0,7,6:T(8,128)(2,1)S(1)} %bitcast.242, f32[6,4,8]{2,1,0:T(4,128)S(1)} %get-tuple-element.564, f32[6,4,8]{2,1,0:T(4,128)S(1)} %get-tuple-element.565, ...), kind=kOutput, calls=%fused_computation.2.clone.1 | convolution fusion | flops 58171392 | bytes 1672711 | tf_op jit(solution)/shard_map/while/body/eval_jaxpr/atgywxd,buhzwvd->watgyxbuhzv/dot_general | solution.py:125
  445.8 5.9 %multiply_convert_fusion.2 = bf16[6,4,8,3,6,2,4,8]{7,2,6,5,4,3,1,0:T(8,128)(2,1)S(1)} fusion(f32[6,4,8,3,6,2,4,8]{7,2,6,5,4,3,1,0:T(8,128)S(1)} %fusion.133, bf16[3,6,2,4,8,128,1,1]{5,4,3,2,1,0,7,6:T(8,128)(2,1)S(1)} %bitcast.242, f32[6,4,8]{2,1,0:T(4,128)S(1)} %get-tuple-element.564, f32[6,4,8]{2,1,0:T(4,128)S(1)} %get-tuple-element.565, ...), kind=kOutput, calls=%fused_computation.2.clone.1 | convolution fusion | flops 58171392 | bytes 1672711 | tf_op jit(solution)/shard_map/while/body/eval_jaxpr/atgywxd,buhzwvd->watgyxbuhzv/dot_general | solution.py:125
  470.4 4.1 collective-permute-start.7
  477.6 4.6 collective-permute-start.10
  483.5 30.5 %collective-permute-done.7 = bf16[6,8,8,1536]{3,2,1,0:T(8,128)(2,1)} collective-permute-done((bf16[6,8,8,1536]{3,2,1,0:T(8,128)(2,1)}, bf16[6,8,8,1536]{3,2,1,0:T(8,128)(2,1)}, u32[]{:S(2)}, u32[]{:S(2)}) %collective-permute-start.7) | collective-permute-done | bytes 1179680 | tf_op jit(solution)/shard_map/ppermute | solution.py:35
  514.0 5.4 collective-permute-done.6
  523.0 19.1 %collective-permute-done.10 = bf16[6,8,8,1536]{3,2,1,0:T(8,128)(2,1)S(1)} collective-permute-done((bf16[6,8,8,1536]{3,2,1,0:T(8,128)(2,1)}, bf16[6,8,8,1536]{3,2,1,0:T(8,128)(2,1)S(1)}, u32[]{:S(2)}, u32[]{:S(2)}) %collective-permute-start.10) | collective-permute-done | bytes 1179680 | tf_op jit(solution)/shard_map/ppermute | solution.py:35
  542.1 5.1 collective-permute-done.9
  551.9 16.5 %all-reduce.2 = (bf16[32,1536]{1,0:T(8,128)(2,1)}, bf16[32,1536]{1,0:T(8,128)(2,1)}) all-reduce(f32[32,1536]{1,0:T(8,128)} %reduce-scatter.3.cloned.1.call-done, f32[32,1536]{1,0:T(8,128)} %reduce-scatter.5.cloned.1.call-done), channel_id=1, replica_groups=mesh['grp'=2,'ta'=4,'ha'=4] {'ha'}, use_global_device_ids=true, to_apply=%region_4.5 | all-reduce | flops 98304 | bytes 589824 | tf_op jit(solution)/shard_map/psum | solution.py:301
  (257 shorter events, 318.1 us)
Async XLA Ops:
  7.2 544.7 %reduce-scatter.3.cloned.1.call-start = ((), (), s32[]{:S(2)}) async-start(), calls=%async_computation.2 | async-start | bytes 983040 | tf_op jit(solution)/shard_map/reduce_scatter | solution.py:298
  7.2 2.4 collective-permute-start.3
  7.7 2.7 collective-permute-start
  13.0 88.7 %collective-permute-start.2 = (bf16[6,8,8,1536]{3,2,1,0:T(8,128)(2,1)}, bf16[6,8,8,1536]{3,2,1,0:T(8,128)(2,1)}, u32[]{:S(2)}, u32[]{:S(2)}) collective-permute-start(bf16[6,8,8,1536]{3,2,1,0:T(8,128)(2,1)} %pad_maximum_fusion.2), channel_id=1, source_target_pairs={{4,0},{8,4},{12,8},{5,1},{9,5},{13,9},{6,2},{10,6},{14,10},{7,3},{... | collective-permute-start | bytes 3538952 | tf_op jit(solution)/shard_map/ppermute | solution.py:27
  14.3 87.4 %collective-permute-start.1 = (bf16[6,8,8,1536]{3,2,1,0:T(8,128)(2,1)}, bf16[6,8,8,1536]{3,2,1,0:T(8,128)(2,1)}, u32[]{:S(2)}, u32[]{:S(2)}) collective-permute-start(bf16[6,8,8,1536]{3,2,1,0:T(8,128)(2,1)} %pad_maximum_fusion.2), channel_id=1, source_target_pairs={{0,4},{4,8},{8,12},{1,5},{5,9},{9,13},{2,6},{6,10},{10,14},{3,7},{... | collective-permute-start | bytes 3538952 | tf_op jit(solution)/shard_map/ppermute | solution.py:24
  21.9 83.0 %collective-permute-start.5 = (bf16[6,8,8,1536]{3,2,1,0:T(8,128)(2,1)}, bf16[6,8,8,1536]{3,2,1,0:T(8,128)(2,1)S(1)}, u32[]{:S(2)}, u32[]{:S(2)}) collective-permute-start(bf16[6,8,8,1536]{3,2,1,0:T(8,128)(2,1)} %pad_maximum_fusion.3), channel_id=1, source_target_pairs={{4,0},{8,4},{12,8},{5,1},{9,5},{13,9},{6,2},{10,6},{14,10},{7,3},{... | collective-permute-start | bytes 3538952 | tf_op jit(solution)/shard_map/ppermute | solution.py:27
  23.2 81.8 %collective-permute-start.4 = (bf16[6,8,8,1536]{3,2,1,0:T(8,128)(2,1)}, bf16[6,8,8,1536]{3,2,1,0:T(8,128)(2,1)}, u32[]{:S(2)}, u32[]{:S(2)}) collective-permute-start(bf16[6,8,8,1536]{3,2,1,0:T(8,128)(2,1)} %pad_maximum_fusion.3), channel_id=1, source_target_pairs={{0,4},{4,8},{8,12},{1,5},{5,9},{9,13},{2,6},{6,10},{10,14},{3,7},{... | collective-permute-start | bytes 3538952 | tf_op jit(solution)/shard_map/ppermute | solution.py:24
  108.9 4.5 copy-start.4
  468.7 8.9 %copy-start.2 = (bf16[3,6,8,8,1536]{4,3,2,1,0:T(8,128)(2,1)}, bf16[3,6,8,8,1536]{4,3,2,1,0:T(8,128)(2,1)S(1)}, u32[]{:S(2)}) copy-start(bf16[3,6,8,8,1536]{4,3,2,1,0:T(8,128)(2,1)S(1)} %get-tuple-element.302) | copy-start | bytes 10616836
  468.7 83.2 %reduce-scatter.5.cloned.1.call-start = ((), (), s32[]{:S(2)}) async-start(), calls=%async_computation.3 | async-start | bytes 983040 | tf_op jit(solution)/shard_map/reduce_scatter | solution.py:299
  468.8 7.1 %copy-start.3 = (bf16[3,6,8,8,1536]{4,3,2,1,0:T(8,128)(2,1)S(1)}, bf16[3,6,8,8,1536]{4,3,2,1,0:T(8,128)(2,1)}, u32[]{:S(2)}) copy-start(bf16[3,6,8,8,1536]{4,3,2,1,0:T(8,128)(2,1)} %get-tuple-element.303) | copy-start | bytes 10616836
  470.4 43.6 %collective-permute-start.7 = (bf16[6,8,8,1536]{3,2,1,0:T(8,128)(2,1)}, bf16[6,8,8,1536]{3,2,1,0:T(8,128)(2,1)}, u32[]{:S(2)}, u32[]{:S(2)}) collective-permute-start(bf16[6,8,8,1536]{3,2,1,0:T(8,128)(2,1)} %get-tuple-element.446), channel_id=1, source_target_pairs={{0,4},{4,8},{8,12},{1,5},{5,9},{9,13},{2,6},{6,10},{10,14},{3,7},{... | collective-permute-start | bytes 3538952 | tf_op jit(solution)/shard_map/ppermute | solution.py:35
  474.6 44.8 %collective-permute-start.6 = (bf16[6,8,8,1536]{3,2,1,0:T(8,128)(2,1)}, bf16[6,8,8,1536]{3,2,1,0:T(8,128)(2,1)}, u32[]{:S(2)}, u32[]{:S(2)}) collective-permute-start(bf16[6,8,8,1536]{3,2,1,0:T(8,128)(2,1)} %get-tuple-element.445), channel_id=1, source_target_pairs={{4,0},{8,4},{12,8},{5,1},{9,5},{13,9},{6,2},{10,6},{14,10},{7,3},{... | collective-permute-start | bytes 3538952 | tf_op jit(solution)/shard_map/ppermute | solution.py:35
  477.6 64.5 %collective-permute-start.10 = (bf16[6,8,8,1536]{3,2,1,0:T(8,128)(2,1)}, bf16[6,8,8,1536]{3,2,1,0:T(8,128)(2,1)S(1)}, u32[]{:S(2)}, u32[]{:S(2)}) collective-permute-start(bf16[6,8,8,1536]{3,2,1,0:T(8,128)(2,1)} %get-tuple-element.444), channel_id=1, source_target_pairs={{0,4},{4,8},{8,12},{1,5},{5,9},{9,13},{2,6},{6,10},{10,14},{3,7},{... | collective-permute-start | bytes 3538952 | tf_op jit(solution)/shard_map/ppermute | solution.py:35
  482.2 65.0 %collective-permute-start.9 = (bf16[6,8,8,1536]{3,2,1,0:T(8,128)(2,1)}, bf16[6,8,8,1536]{3,2,1,0:T(8,128)(2,1)}, u32[]{:S(2)}, u32[]{:S(2)}) collective-permute-start(bf16[6,8,8,1536]{3,2,1,0:T(8,128)(2,1)} %get-tuple-element.443), channel_id=1, source_target_pairs={{4,0},{8,4},{12,8},{5,1},{9,5},{13,9},{6,2},{10,6},{14,10},{7,3},{... | collective-permute-start | bytes 3538952 | tf_op jit(solution)/shard_map/ppermute | solution.py:35
  523.0 45.4 %collective-permute-start.8 = (f32[6,4,8,1536]{3,2,1,0:T(8,128)}, f32[6,4,8,1536]{3,2,1,0:T(8,128)}, u32[]{:S(2)}, u32[]{:S(2)}) collective-permute-start(f32[6,4,8,1536]{3,2,1,0:T(8,128)} %slice_select_fusion.1), channel_id=1, source_target_pairs={{0,1},{1,0},{2,3},{3,2},{4,5},{5,4},{6,7},{7,6},{8,9},{9,8},{10,11... | collective-permute-start | bytes 3538952 | tf_op jit(solution)/shard_map/ppermute | solution.py:16
  549.3 1.4 copy-start
  551.9 19.0 %collective-permute-start.11 = (f32[6,4,8,1536]{3,2,1,0:T(8,128)}, f32[6,4,8,1536]{3,2,1,0:T(8,128)S(1)}, u32[]{:S(2)}, u32[]{:S(2)}) collective-permute-start(f32[6,4,8,1536]{3,2,1,0:T(8,128)} %slice_select_fusion), channel_id=1, source_target_pairs={{0,1},{1,0},{2,3},{3,2},{4,5},{5,4},{6,7},{7,6},{8,9},{9,8},{10,11... | collective-permute-start | bytes 3538952 | tf_op jit(solution)/shard_map/ppermute | solution.py:16
  568.4 2.5 copy-start.1
Sparse Core Ops, SparseCore 0:
  468.9 34.8 reduce-scatter.2
  506.0 34.7 reduce-scatter.4
where the time goes:
time: 587 us; the launch traced here: 579 us
  matrix products  289 us (49%)
  blocking collectives  85.8 us (15%)
  waiting for transfers between devices  62.7 us (11%)
  local copies, waits for them, and re-layouts  54.2 us (9%)
  other arithmetic  37.2 us (6%)
  starting transfers between devices  26.7 us (5%)
  between operations  14.2 us (2%)
  loops' own time  8.61 us (1%)
    dot_general x12, matrix products, pair_grads(): jnp.einsum(pattern, grad_grid, value_grid, preferred_element_type=jnp.flo...  71.2 us
    ppermute x4, waiting for transfers between devices, passed_along(): return lax.ppermute(block, axis, route)  60.1 us
    all_gather x1, blocking collectives, per_device(): lax.all_gather(text_keys, 'ta', axis=0, tiled=True)  51.9 us
    dot_general x12, matrix products, pair_grads(): jnp.einsum('watgyxbuhzv,atgywxd->buhzwvagd', prob_data, grad_grid, prefer...  43.8 us
    dot_general x12, matrix products, pair_grads(): jnp.einsum(pattern, query_grid, key_grid, preferred_element_type=jnp.floa...  33.7 us
    dot_general x12, matrix products, pair_grads(): jnp.einsum('watgyxbuhzv,atgywxd->buhzwvagd', score_grad, query_grid, pref...  33.4 us
    dot_general x12, matrix products, pair_grads(): jnp.einsum('watgyxbuhzv,buhzwvd->atgywxbhd', score_grad, key_grid, prefer...  25.6 us
    dot_general x12, matrix products, text_grads(): jnp.einsum('wtyxj,tywxd->jd', score_grad, query_grid, preferred_element_t...  19.8 us
  transfers between devices with their start and end apart: 14, of which 6 were waited for; matrix products, arithmetic and copies ran while one was open for 4% of the time, Pallas kernels for 0%

commit v1 on v0

v1 whole, which is shorter than its diff:
```python
import functools

import jax
import jax.numpy as jnp
from jax import lax
from jax.experimental import pallas as pl
from jax.experimental.pallas import tpu as pltpu
from jax.sharding import PartitionSpec as P

LOG2E = 1.4426950408889634
HIDDEN_LSE = 1e30
MESH_ID = pl.DeviceIdType.MESH
NT = (((1,), (1,)), ((), ()))
NN = (((1,), (0,)), ((), ()))
TN = (((0,), (0,)), ((), ()))


def dot(a, b, dims):
    return lax.dot_general(a, b, dims, preferred_element_type=jnp.float32)


def kernel(
    tiles,
    heads,
    size,
    q_in,
    g_in,
    k_in,
    v_in,
    stat_in,
    text_k,
    text_v,
    length,
    reach,
    q_out,
    k_out,
    v_out,
    tk_out,
    tv_out,
    qw,
    gw,
    kw,
    vw,
    sw,
    st,
    ak,
    av,
    dq,
    dk,
    rq,
    rk,
    local_sem,
    pair_send,
    pair_recv,
    stat_send,
    stat_recv,
    far_send,
    far_recv,
    term_send,
    term_recv,
    kv_send,
    kv_recv,
):
    rows = q_in.shape[0]
    cols = heads * size
    scaling = size ** (-0.5)
    grp = lax.axis_index("grp")
    t = lax.axis_index("ta")
    ha = lax.axis_index("ha")
    c = lax.rem(ha, 2)
    o = 1 - c
    base = ha - c
    partner = (grp, t, base + o)
    has = (t > 0, t < tiles - 1)
    near = (t - 1, t + 1)

    def group(index):
        return pl.ds(pl.multiple_of(index * cols, 128), cols)

    def head(j):
        return pl.ds(pl.multiple_of(j * size, 128), size)

    def group_head(index, j):
        return pl.ds(pl.multiple_of(index * cols + j * size, 128), size)

    barrier = pltpu.get_barrier_semaphore()
    pl.semaphore_signal(barrier, inc=1, device_id=partner, device_id_type=MESH_ID)
    for d in range(2):

        @pl.when(has[d])
        def _():
            for cc in range(2):
                pl.semaphore_signal(
                    barrier, inc=1, device_id=(grp, near[d], base + cc), device_id_type=MESH_ID
                )

    count = 1 + 2 * jnp.where(t > 0, 1, 0) + 2 * jnp.where(t < tiles - 1, 1, 0)
    pl.semaphore_wait(barrier, count)

    def far(d, cc, a, j):
        src = (q_in, g_in)[a]
        dst = (qw, gw)[a]
        return pltpu.make_async_remote_copy(
            src_ref=src.at[:, group_head(cc, j)],
            dst_ref=dst.at[2 - d, c, :, head(j)],
            send_sem=far_send.at[d, cc, a, j],
            recv_sem=far_recv.at[1 - d, c, a, j],
            device_id=(grp, near[d], base + cc),
            device_id_type=MESH_ID,
        )

    def far_wait(d, b, a, j):
        dst = (qw, gw)[a].at[1 + d, b, :, head(j)]
        pltpu.make_async_copy(dst, dst, far_recv.at[d, b, a, j]).wait()

    def stat_far(d, cc):
        return pltpu.make_async_remote_copy(
            src_ref=stat_in.at[cc],
            dst_ref=sw.at[2 - d, c],
            send_sem=stat_send.at[1 + d, cc],
            recv_sem=stat_recv.at[2 - d, c],
            device_id=(grp, near[d], base + cc),
            device_id_type=MESH_ID,
        )

    def pair(a):
        src = (q_in, g_in, k_in, v_in)[a]
        dst = (qw.at[0, c], gw.at[0, c], kw.at[c], vw.at[c])[a]
        return pltpu.make_async_remote_copy(
            src_ref=src.at[:, group(o)],
            dst_ref=dst,
            send_sem=pair_send.at[a],
            recv_sem=pair_recv.at[a],
            device_id=partner,
            device_id_type=MESH_ID,
        )

    def own(a):
        src = (q_in, g_in, k_in, v_in)[a]
        dst = (qw.at[0, c], gw.at[0, c], kw.at[c], vw.at[c])[a]
        return pltpu.make_async_copy(src.at[:, group(c)], dst, local_sem.at[a])

    stat_pair = pltpu.make_async_remote_copy(
        src_ref=stat_in.at[o],
        dst_ref=sw.at[0, c],
        send_sem=stat_send.at[0, 0],
        recv_sem=stat_recv.at[0, 0],
        device_id=partner,
        device_id_type=MESH_ID,
    )

    stat_pair.start()
    for a in range(4):
        pair(a).start()
        own(a).start()
    for d in range(2):

        @pl.when(has[d])
        def _():
            for cc in range(2):
                stat_far(d, cc).start()

    def send_far(j, carry):
        for d in range(2):

            @pl.when(has[d])
            def _():
                for a in range(2):
                    for cc in range(2):
                        far(d, cc, a, j).start()

        return carry

    lax.fori_loop(0, heads, send_far, 0)

    for d in range(2):

        @pl.when(jnp.logical_not(has[d]))
        def _():
            rq[1 + d] = jnp.zeros_like(rq[1 + d])

    for a in range(4):
        own(a).wait()
        pair(a).wait_recv()
    stat_pair.wait_recv()
    st[0] = stat_in[c] + sw[0, o]

    def term(s, b, j):
        target = partner if s == 0 else (grp, near[s - 1], base + b)
        slot = (0, 2, 1)[s]
        return pltpu.make_async_remote_copy(
            src_ref=dq.at[s, b, :, head(j)],
            dst_ref=rq.at[slot, c, :, head(j)],
            send_sem=term_send.at[s, 0 if s == 0 else b, j],
            recv_sem=term_recv.at[slot, c, j],
            device_id=target,
            device_id_type=MESH_ID,
        )

    def term_wait(slot, group_index, j):
        dst = rq.at[slot, group_index, :, head(j)]
        pltpu.make_async_copy(dst, dst, term_recv.at[slot, group_index, j]).wait()

    def kv(a, j):
        return pltpu.make_async_remote_copy(
            src_ref=dk.at[a, o, :, head(j)],
            dst_ref=rk.at[a, :, head(j)],
            send_sem=kv_send.at[a, j],
            recv_sem=kv_recv.at[a, j],
            device_id=partner,
            device_id_type=MESH_ID,
        )

    def both(ref, j):
        return ref[:, :, head(j)].reshape(2 * rows, size)

    def grads(q, g, k, v, lse, out_dot, ok):
        weight = jnp.exp2(dot(k, q, NT) * (scaling * LOG2E) - lse)
        if ok is not None:
            weight = jnp.where(ok, weight, 0.0)
        score = (weight * (dot(v, g, NT) - out_dot) * scaling).astype(jnp.bfloat16)
        prob = weight.astype(jnp.bfloat16)
        return dot(score, k, TN), dot(score, q, NN), dot(prob, g, NN)

    text_ok = lax.broadcasted_iota(jnp.int32, (text_k.shape[0], 1), 0) < length[0]

    def near_step(j, carry):
        q, g = both(qw.at[0], j), both(gw.at[0], j)
        lse, out_dot = st[0, pl.ds(j, 1), :], st[0, pl.ds(8 + j, 1), :]
        dq_own, dk_own, dv_own = grads(q, g, both(kw, j), both(vw, j), lse, out_dot, None)
        tk, tv = text_k[:, group_head(c, j)], text_v[:, group_head(c, j)]
        dq_text, dk_text, dv_text = grads(q, g, tk, tv, lse, out_dot, text_ok)
        ak[:, head(j)] = dk_own
        av[:, head(j)] = dv_own
        tk_out[:, head(j)] = dk_text
        tv_out[:, head(j)] = dv_text
        total = (dq_own + dq_text).astype(jnp.bfloat16)
        dq[0, :, :, head(j)] = total.reshape(2, rows, size)
        term(0, o, j).start()
        return carry

    lax.fori_loop(0, heads, near_step, 0)

    for d in range(2):

        @pl.when(has[d])
        def _():
            for b in range(2):
                dst = sw.at[1 + d, b]
                pltpu.make_async_copy(dst, dst, stat_recv.at[1 + d, b]).wait()
            st[1 + d] = sw[1 + d, 0] + sw[1 + d, 1]

    def far_step(j, carry):
        for d in range(2):

            @pl.when(has[d])
            def _():
                for a in range(2):
                    for b in range(2):
                        far_wait(d, b, a, j)
                seen = reach[c * heads + j, 1 - d] >= 1
                lse = st[1 + d, pl.ds(j, 1), :] + jnp.where(seen, 0.0, HIDDEN_LSE)
                out_dot = st[1 + d, pl.ds(8 + j, 1), :]
                dq_far, dk_far, dv_far = grads(
                    both(qw.at[1 + d], j),
                    both(gw.at[1 + d], j),
                    both(kw, j),
                    both(vw, j),
                    lse,
                    out_dot,
                    None,
                )
                ak[:, head(j)] += dk_far
                av[:, head(j)] += dv_far
                dq[1 + d, :, :, head(j)] = (
                    dq_far.astype(jnp.bfloat16).reshape(2, rows, size)
                )
                for b in range(2):
                    term(1 + d, b, j).start()

        dk[0, :, :, head(j)] = (
            ak[:, head(j)].astype(jnp.bfloat16).reshape(2, rows, size)
        )
        dk[1, :, :, head(j)] = av[:, head(j)].astype(jnp.bfloat16).reshape(2, rows, size)
        for a in range(2):
            kv(a, j).start()
        return carry

    lax.fori_loop(0, heads, far_step, 0)

    k_out[:, group(c)] = dk[0, c]
    v_out[:, group(c)] = dk[1, c]

    def finish(j, carry):
        for a in range(2):
            kv(a, j).wait()
        term(0, o, j).wait_send()
        term_wait(0, o, j)
        for d in range(2):

            @pl.when(has[d])
            def _():
                for b in range(2):
                    term_wait(1 + d, b, j)
                    term(1 + d, b, j).wait_send()
                    for a in range(2):
                        far(d, b, a, j).wait_send()

        return carry

    lax.fori_loop(0, heads, finish, 0)
    stat_pair.wait_send()
    for a in range(4):
        pair(a).wait_send()
    for d in range(2):

        @pl.when(has[d])
        def _():
            for cc in range(2):
                stat_far(d, cc).wait_send()

    k_out[:, group(o)] = rk[0]
    v_out[:, group(o)] = rk[1]

    def total(own_part, index):
        return (
            own_part.astype(jnp.float32)
            + rq[1, index].astype(jnp.float32)
            + rq[2, index].astype(jnp.float32)
        ).astype(q_out.dtype)

    q_out[:, group(c)] = total(dq[0, c], c)
    q_out[:, group(o)] = total(rq[0, o], o)


def per_device(
    queries,
    key_rows,
    value_rows,
    out_grad,
    logsumexp,
    out_dot,
    text_keys,
    text_values,
    text_length,
    window_reach,
):
    shape = queries.shape
    hidden = shape[3]
    rows = shape[0] * shape[1] * shape[2]
    head_count = logsumexp.shape[3]
    size = hidden // head_count
    heads = head_count // 2
    cols = heads * size
    tiles = lax.axis_size("ta")
    half = lax.axis_index("ha") % 2

    def stat(values):
        turned = values.reshape(rows, head_count).T.reshape(2, heads, rows)
        return jnp.pad(turned, ((0, 0), (0, 8 - heads), (0, 0)))

    stats = jnp.concatenate([stat(logsumexp * LOG2E), stat(out_dot)], axis=1)
    empty = jnp.zeros_like(stats)
    stats = jnp.where(
        half == 0,
        jnp.concatenate([stats, empty], axis=2),
        jnp.concatenate([empty, stats], axis=2),
    )
    text_k = lax.all_gather(text_keys, "ta", axis=0, tiled=True)
    text_v = lax.all_gather(text_values, "ta", axis=0, tiled=True)
    text_count = text_k.shape[0]
    vmem = pl.BlockSpec(memory_space=pltpu.VMEM)
    smem = pl.BlockSpec(memory_space=pltpu.SMEM)
    bf16, f32 = jnp.bfloat16, jnp.float32
    dma = pltpu.SemaphoreType.DMA
    query_grad, key_grad, value_grad, key_text, value_text = pl.pallas_call(
        functools.partial(kernel, tiles, heads, size),
        out_shape=[jax.ShapeDtypeStruct((rows, hidden), bf16)] * 3
        + [jax.ShapeDtypeStruct((text_count, cols), f32)] * 2,
        in_specs=[vmem] * 7 + [smem] * 2,
        out_specs=[vmem] * 5,
        scratch_shapes=[
            pltpu.VMEM((3, 2, rows, cols), bf16),
            pltpu.VMEM((3, 2, rows, cols), bf16),
            pltpu.VMEM((2, rows, cols), bf16),
            pltpu.VMEM((2, rows, cols), bf16),
            pltpu.VMEM((3, 2, 16, 2 * rows), f32),
            pltpu.VMEM((3, 16, 2 * rows), f32),
            pltpu.VMEM((2 * rows, cols), f32),
            pltpu.VMEM((2 * rows, cols), f32),
            pltpu.VMEM((3, 2, rows, cols), bf16),
            pltpu.VMEM((2, 2, rows, cols), bf16),
            pltpu.VMEM((3, 2, rows, cols), bf16),
            pltpu.VMEM((2, rows, cols), bf16),
            dma((4,)),
            dma((4,)),
            dma((4,)),
            dma((3, 2)),
            dma((3, 2)),
            dma((2, 2, 2, heads)),
            dma((2, 2, 2, heads)),
            dma((3, 2, heads)),
            dma((3, 2, heads)),
            dma((2, heads)),
            dma((2, heads)),
        ],
        compiler_params=pltpu.CompilerParams(
            collective_id=0, has_side_effects=True, vmem_limit_bytes=48 * 1024 * 1024
        ),
        cost_estimate=pl.CostEstimate(
            flops=20 * rows * rows * 7 * hidden, bytes_accessed=16 * rows * hidden, transcendentals=0
        ),
    )(
        queries.reshape(rows, hidden),
        out_grad.reshape(rows, hidden),
        key_rows.reshape(rows, hidden),
        value_rows.reshape(rows, hidden),
        stats,
        text_k,
        text_v,
        text_length,
        window_reach,
    )

    def text_total(part):
        whole = jnp.zeros((2, text_count, cols), f32)
        whole = lax.dynamic_update_slice_in_dim(whole, part[None], half, 0)
        whole = whole.transpose(1, 0, 2).reshape(text_count, hidden)
        return lax.psum_scatter(whole, "ta", scatter_dimension=0, tiled=True)

    totals = lax.psum((text_total(key_text), text_total(value_text)), "ha")
    return (
        query_grad.reshape(shape),
        key_grad.reshape(shape),
        value_grad.reshape(shape),
        totals[0].astype(bf16),
        totals[1].astype(bf16),
    )


def solution(mesh):
    block = P(("grp", "ta"), "ha", None, None)
    text = P(("grp", "ta"), None)
    return jax.shard_map(
        per_device,
        mesh=mesh,
        in_specs=(block,) * 6 + (text, text, P("grp"), P()),
        out_specs=(block,) * 3 + (text, text),
        check_vma=False,
    )
```

time: 587 us -> 171 us (0.29); the launches traced: 579 us -> 171 us
  matrix products: 289 us -> 0 us
  Pallas kernels: 0 us -> 44.4 us
  blocking collectives: 85.8 us -> 47.7 us
  other arithmetic: 37.2 us -> 0.99 us
  local copies, waits for them, and re-layouts: 54.2 us -> 21 us
  starting transfers between devices: 26.7 us -> 0.08 us
  waiting for transfers between devices: 62.7 us -> 41.9 us
  loops' own time: 8.61 us -> 0 us
    dot_general x120 -> x0, matrix products: 289 us -> none  [the longest x12 71.2 us: pair_grads(): jnp.einsum(pattern, grad_grid, value_grid, preferred_element_type=jnp.flo...]
    ppermute x12 -> x0, waiting for transfers between devices: 62.7 us -> none  [the longest x4 60.1 us: passed_along(): return lax.ppermute(block, axis, route)]
    pallas_call x0 -> x1, Pallas kernels: none -> 44.4 us  [per_device(): pl.pallas_call(functools.partial(kernel, tiles, heads, size), out_shape=[...]
    reduce_scatter x2, waiting for transfers between devices: 0.01 us -> 41.9 us  [text_total(): return lax.psum_scatter(whole, 'ta', scatter_dimension=0, tiled=True)]
    all_gather x2, blocking collectives: 69.2 us -> 32 us  [the longest x1 16.4 us: per_device(): text_k = lax.all_gather(text_keys, 'ta', axis=0, tiled=True)]
    ppermute x12 -> x0, starting transfers between devices: 26.6 us -> none  [the longest x2 12.1 us: padded(): lax.ppermute(lax.slice_in_dim(block, block.shape[dim] - width, None, axis...]
    dynamic_slice x24 -> x0, local copies, waits for them, and re-layouts: 21.3 us -> none  [the longest x12 13.3 us: column(): lax.dynamic_slice_in_dim(array, head_index * head_size, head_size, array....]
    sub x12 -> x0, local copies, waits for them, and re-layouts: 8.82 us -> none  [pair_grads(): prob_grad - dot_grid]
  transfers between devices with their start and end apart: 14 -> 2, of which waited for: 6 -> 2; matrix products, arithmetic and copies ran while one was open for 4% -> 4% of each run, Pallas kernels for 0% -> 0%
where the time goes in v1:
time: 171 us
  blocking collectives  47.7 us (28%)
  Pallas kernels  44.4 us (26%)
  waiting for transfers between devices  41.9 us (25%)
  local copies, waits for them, and re-layouts  21 us (12%)
  between operations  14.8 us (9%)
    pallas_call x1, Pallas kernels, per_device(): pl.pallas_call(functools.partial(kernel, tiles, heads, size), out_shape=[...  44.4 us
    reduce_scatter x2, waiting for transfers between devices, text_total(): return lax.psum_scatter(whole, 'ta', scatter_dimension=0, tiled=True)  41.9 us
    all_gather x1, blocking collectives, per_device(): text_k = lax.all_gather(text_keys, 'ta', axis=0, tiled=True)  16.4 us
    all_gather x1, blocking collectives, per_device(): text_v = lax.all_gather(text_values, 'ta', axis=0, tiled=True)  15.7 us
    psum x1, blocking collectives, per_device(): totals = lax.psum((text_total(key_text), text_total(value_text)), 'ha')  15.6 us
    dynamic_update_slice x2, local copies, waits for them, and re-layouts, text_total(): whole = lax.dynamic_update_slice_in_dim(whole, part[None], half, 0)  11.1 us
    unnamed x22, local copies, waits for them, and re-layouts  8.46 us
  transfers between devices with their start and end apart: 2, of which 2 were waited for; matrix products, arithmetic and copies ran while one was open for 4% of the time, Pallas kernels for 0%

profile of v1, /device:TPU:0, one launch (start us, length us, event | category | flops | bytes accessed | tf_op | source)
XLA Modules:
  0.0 170.9 jit_solution(1109574108069643201)
XLA Ops:
  7.2 0.9 broadcast_multiply_fusion
  8.2 0.8 copy-done.4
  9.1 16.4 %all_gather.6.text_k = bf16[128,1536]{1,0:T(8,128)(2,1)S(1)} all-gather(bf16[32,1536]{1,0:T(8,128)(2,1)S(1)} %copy-done.5), channel_id=1, replica_groups=mesh['grp'=2,'ta'=4,'ha'=4] {'ta'}, dimensions={0}, use_global_device_ids=true | all-gather | bytes 491520 | tf_op jit(solution)/shard_map/all_gather | solution.py:369
  25.5 15.7 %all_gather.7.text_v = bf16[128,1536]{1,0:T(8,128)(2,1)S(1)} all-gather(bf16[32,1536]{1,0:T(8,128)(2,1)S(1)} %copy-done.6), channel_id=1, replica_groups=mesh['grp'=2,'ta'=4,'ha'=4] {'ta'}, dimensions={0}, use_global_device_ids=true | all-gather | bytes 491520 | tf_op jit(solution)/shard_map/all_gather | solution.py:370
  41.2 0.1 copy.22.reach
  41.9 0.1 pad_select_fusion.stat_in
  42.0 1.1 copy-done.1
  43.1 1.1 copy-done.2
  44.2 1.1 copy-done.3
  45.2 44.4 %shard_map.137 = (bf16[192,1536]{1,0:T(8,128)(2,1)S(1)}, bf16[192,1536]{1,0:T(8,128)(2,1)S(1)}, bf16[192,1536]{1,0:T(8,128)(2,1)S(1)}, f32[128,768]{1,0:T(8,128)S(1)}, f32[128,768]{1,0:T(8,128)S(1)}) custom-call(bf16[192,1536]{1,0:T(8,128)(2,1)S(1)} %bitcast.24, bf16[192,1536]{1,0:T(8,128)(2,1)S(1)} %bitcast.25, bf16[192,1536]{1,0:T(8,128)(2,1)S(1)} %bitcast.26, ...), custom_call_target="tpu_custom_call" | custom-call | flops 7927234560 | bytes 4718592 | tf_op jit(solution)/shard_map/pallas_call | solution.py:376
  89.6 0.4 copy.23
  90.1 0.2 broadcast.12.clone
  90.3 5.6 %dynamic_update_slice.6 = f32[2,128,768]{2,0,1:T(2,128)S(1)} dynamic-update-slice(f32[2,128,768]{2,0,1:T(2,128)S(1)} %broadcast.12.clone, f32[1,128,768]{2,0,1:T(1,128)S(1)} %copy.23, s32[]{:T(128)S(6)} %select_n.22, s32[]{:T(128)} %constant.19.clone.1, s32[]{:T(128)} %constant.19.clone.1) | dynamic-update-slice | bytes 786436 | tf_op jit(solution)/shard_map/dynamic_update_slice | solution.py:427
  95.8 0.9 copy.25
  96.9 0.4 copy.24
  97.3 0.2 broadcast.12.clone.1
  97.5 5.6 %dynamic_update_slice.7 = f32[2,128,768]{2,0,1:T(2,128)S(1)} dynamic-update-slice(f32[2,128,768]{2,0,1:T(2,128)S(1)} %broadcast.12.clone.1, f32[1,128,768]{2,0,1:T(1,128)S(1)} %copy.24, s32[]{:T(128)S(6)} %select_n.22, s32[]{:T(128)} %constant.19.clone.1, s32[]{:T(128)} %constant.19.clone.1) | dynamic-update-slice | bytes 786436 | tf_op jit(solution)/shard_map/dynamic_update_slice | solution.py:427
  103.1 1.0 copy.26
  104.0 17.0 %reduce-scatter.3.cloned.1.call-done = f32[32,1536]{1,0:T(8,128)} async-done(((f32[128,1536]{1,0:T(8,128)}), f32[32,1536]{1,0:T(8,128)}) %reduce-scatter.3.cloned.1.call-update) | async-done | bytes 196624 | tf_op jit(solution)/shard_map/reduce_scatter | solution.py:429
  121.1 24.9 %reduce-scatter.5.cloned.1.call-done = f32[32,1536]{1,0:T(8,128)} async-done(((f32[128,1536]{1,0:T(8,128)}), f32[32,1536]{1,0:T(8,128)}) %reduce-scatter.5.cloned.1.call-update) | async-done | bytes 196624 | tf_op jit(solution)/shard_map/reduce_scatter | solution.py:429
  145.9 15.6 %all-reduce.6 = (bf16[32,1536]{1,0:T(8,128)(2,1)}, bf16[32,1536]{1,0:T(8,128)(2,1)}) all-reduce(f32[32,1536]{1,0:T(8,128)} %reduce-scatter.3.cloned.1.call-done, f32[32,1536]{1,0:T(8,128)} %reduce-scatter.5.cloned.1.call-done), channel_id=1, replica_groups=mesh['grp'=2,'ta'=4,'ha'=4] {'ha'}, use_global_device_ids=true, to_apply=%region_1.2 | all-reduce | flops 98304 | bytes 589824 | tf_op jit(solution)/shard_map/psum | solution.py:431
  161.6 0.8 copy.37
  162.4 0.8 copy.38
  163.2 0.8 copy.39
  (21 shorter events, 0.3 us)
Async XLA Ops:
  7.2 113.9 %reduce-scatter.3.cloned.1.call-start = ((), (), s32[]{:S(2)}) async-start(), calls=%async_computation.2 | async-start | bytes 983040 | tf_op jit(solution)/shard_map/reduce_scatter | solution.py:429
  8.1 0.9 copy-start.4
  8.2 0.9 copy-start.5
  9.0 16.5 %copy-start.6 = (bf16[32,1536]{1,0:T(8,128)(2,1)S(1)}, bf16[32,1536]{1,0:T(8,128)(2,1)}, u32[]{:S(2)}) copy-start(bf16[32,1536]{1,0:T(8,128)(2,1)} %param.17) | copy-start | bytes 294916
  9.1 32.9 %copy-start = (bf16[6,4,8,1536]{3,2,1,0:T(8,128)(2,1)S(1)}, bf16[6,4,8,1536]{3,2,1,0:T(8,128)(2,1)}, u32[]{:S(2)}) copy-start(bf16[6,4,8,1536]{3,2,1,0:T(8,128)(2,1)} %param.10) | copy-start | bytes 1769476
  25.5 15.7 %copy-start.7 = (s32[12,2]{0,1:T(2,128)S(1)}, s32[12,2]{0,1:T(2,128)}, u32[]{:S(2)}) copy-start(s32[12,2]{0,1:T(2,128)} %param.19) | copy-start | bytes 292
  42.0 1.1 copy-start.1
  43.1 1.1 copy-start.2
  44.1 1.1 copy-start.3
  96.8 49.1 %reduce-scatter.5.cloned.1.call-start = ((), (), s32[]{:S(2)}) async-start(), calls=%async_computation.3 | async-start | bytes 983040 | tf_op jit(solution)/shard_map/reduce_scatter | solution.py:429
Sparse Core Ops, SparseCore 0:
  96.9 24.0 reduce-scatter.2
  123.4 22.5 reduce-scatter.4

commit v2 on v1

--- a/solution.py
+++ b/solution.py
@@ -23,6 +23,7 @@
     tiles,
     heads,
     size,
+    fused,
     q_in,
     g_in,
     k_in,
@@ -60,6 +61,8 @@
     term_recv,
     kv_send,
     kv_recv,
+    aq,
+    *text_scratch,
 ):
     rows = q_in.shape[0]
     cols = heads * size
@@ -95,7 +98,90 @@
                 )
 
     count = 1 + 2 * jnp.where(t > 0, 1, 0) + 2 * jnp.where(t < tiles - 1, 1, 0)
+    if fused:
+        (tw, tp, tb, tr, tf, tsb, tz, tfb, to) = text_scratch[:9]
+        (tg_send, tg_recv, tx_send, tx_recv, xr_sem, zt_send, zt_recv, fin_send, fin_recv) = (
+            text_scratch[9:]
+        )
+        half_rows = tw.shape[3]
+        p = lax.div(ha, 2)
+        across = (grp, t, lax.rem(ha + 2, 4))
+        diagonal = (grp, t, 2 * (1 - p) + o)
+        for place in (across, diagonal):
+            pl.semaphore_signal(barrier, inc=1, device_id=place, device_id_type=MESH_ID)
+        for tt in range(tiles):
+
+            @pl.when((t - tt) * (t - tt) > 1)
+            def _():
+                pl.semaphore_signal(
+                    barrier, inc=1, device_id=(grp, tt, ha), device_id_type=MESH_ID
+                )
+
+        count = tiles + 2 + jnp.where(t > 0, 1, 0) + jnp.where(t < tiles - 1, 1, 0)
     pl.semaphore_wait(barrier, count)
+
+    def elsewhere(action):
+        for tt in range(tiles):
+
+            @pl.when(t != tt)
+            def _():
+                action(tt)
+
+    if fused:
+
+        def text_gather(a, tt):
+            return pltpu.make_async_remote_copy(
+                src_ref=(text_k, text_v)[a].at[
+                    pl.ds(pl.multiple_of(p * half_rows, half_rows), half_rows), group(c)
+                ],
+                dst_ref=tw.at[t, p, a],
+                send_sem=tg_send.at[a, tt],
+                recv_sem=tg_recv.at[a, t],
+                device_id=(grp, tt, ha),
+                device_id_type=MESH_ID,
+            )
+
+        def text_across(tt):
+            return pltpu.make_async_remote_copy(
+                src_ref=tw.at[tt, p],
+                dst_ref=tw.at[tt, p],
+                send_sem=tx_send.at[tt],
+                recv_sem=tx_recv.at[tt],
+                device_id=across,
+                device_id_type=MESH_ID,
+            )
+
+        sum_across = pltpu.make_async_remote_copy(
+            src_ref=tb.at[1 - p],
+            dst_ref=tr,
+            send_sem=xr_sem.at[0],
+            recv_sem=xr_sem.at[1],
+            device_id=across,
+            device_id_type=MESH_ID,
+        )
+
+        def sum_along(tt):
+            return pltpu.make_async_remote_copy(
+                src_ref=tsb.at[tt],
+                dst_ref=tz.at[t],
+                send_sem=zt_send.at[tt],
+                recv_sem=zt_recv.at[t],
+                device_id=(grp, tt, ha),
+                device_id_type=MESH_ID,
+            )
+
+        def spread(k):
+            return pltpu.make_async_remote_copy(
+                src_ref=tfb,
+                dst_ref=to.at[c, p],
+                send_sem=fin_send.at[k],
+                recv_sem=fin_recv.at[c, p],
+                device_id=(partner, across, diagonal)[k],
+                device_id_type=MESH_ID,
+            )
+
+        def arrival(ref, sem):
+            pltpu.make_async_copy(ref, ref, sem).wait()
 
     def far(d, cc, a, j):
         src = (q_in, g_in)[a]
@@ -150,6 +236,13 @@
     )
 
     stat_pair.start()
+    if fused:
+
+        def send_text(tt):
+            for a in range(2):
+                text_gather(a, tt).start()
+
+        elsewhere(send_text)
     for a in range(4):
         pair(a).start()
         own(a).start()
@@ -178,6 +271,18 @@
         @pl.when(jnp.logical_not(has[d]))
         def _():
             rq[1 + d] = jnp.zeros_like(rq[1 + d])
+
+    if fused:
+        for hh in range(2):
+            for a in range(2):
+                tw[t, hh, a] = (text_k, text_v)[a][hh * half_rows : (hh + 1) * half_rows, group(c)]
+
+        def forward_text(tt):
+            for a in range(2):
+                arrival(tw.at[tt, p, a], tg_recv.at[a, tt])
+            text_across(tt).start()
+
+        elsewhere(forward_text)
 
     for a in range(4):
         own(a).wait()
@@ -222,24 +327,52 @@
         prob = weight.astype(jnp.bfloat16)
         return dot(score, k, TN), dot(score, q, NN), dot(prob, g, NN)
 
-    text_ok = lax.broadcasted_iota(jnp.int32, (text_k.shape[0], 1), 0) < length[0]
+    text_count = tiles * text_k.shape[0] if fused else text_k.shape[0]
+    text_ok = lax.broadcasted_iota(jnp.int32, (text_count, 1), 0) < length[0]
+
+    def stats(s, j):
+        return st[s, pl.ds(j, 1), :], st[s, pl.ds(8 + j, 1), :]
 
     def near_step(j, carry):
         q, g = both(qw.at[0], j), both(gw.at[0], j)
-        lse, out_dot = st[0, pl.ds(j, 1), :], st[0, pl.ds(8 + j, 1), :]
+        lse, out_dot = stats(0, j)
         dq_own, dk_own, dv_own = grads(q, g, both(kw, j), both(vw, j), lse, out_dot, None)
-        tk, tv = text_k[:, group_head(c, j)], text_v[:, group_head(c, j)]
-        dq_text, dk_text, dv_text = grads(q, g, tk, tv, lse, out_dot, text_ok)
         ak[:, head(j)] = dk_own
         av[:, head(j)] = dv_own
-        tk_out[:, head(j)] = dk_text
-        tv_out[:, head(j)] = dv_text
-        total = (dq_own + dq_text).astype(jnp.bfloat16)
+        aq[:, head(j)] = dq_own
+        return carry
+
+    def text_step(j, carry):
+        q, g = both(qw.at[0], j), both(gw.at[0], j)
+        lse, out_dot = stats(0, j)
+        if fused:
+            tk = tw[:, :, 0, :, head(j)].reshape(text_count, size)
+            tv = tw[:, :, 1, :, head(j)].reshape(text_count, size)
+        else:
+            tk, tv = text_k[:, group_head(c, j)], text_v[:, group_head(c, j)]
+        dq_text, dk_text, dv_text = grads(q, g, tk, tv, lse, out_dot, text_ok)
+        if fused:
+            for a, part in enumerate((dk_text, dv_text)):
+                for tt in range(tiles):
+                    for hh in range(2):
+                        low = (2 * tt + hh) * half_rows
+                        piece = part[low : low + half_rows]
+                        tp[hh, tt, a, :, head(j)] = piece
+                        tb[hh, tt, a, :, head(j)] = piece.astype(jnp.bfloat16)
+        else:
+            tk_out[:, head(j)] = dk_text
+            tv_out[:, head(j)] = dv_text
+        total = (aq[:, head(j)] + dq_text).astype(jnp.bfloat16)
         dq[0, :, :, head(j)] = total.reshape(2, rows, size)
         term(0, o, j).start()
         return carry
 
     lax.fori_loop(0, heads, near_step, 0)
+    if fused:
+        elsewhere(lambda tt: arrival(tw.at[tt, 1 - p], tx_recv.at[tt]))
+    lax.fori_loop(0, heads, text_step, 0)
+    if fused:
+        sum_across.start()
 
     for d in range(2):
 
@@ -286,7 +419,26 @@
             kv(a, j).start()
         return carry
 
-    lax.fori_loop(0, heads, far_step, 0)
+    early = 2
+    lax.fori_loop(0, early, far_step, 0)
+    if fused:
+        sum_across.wait_recv()
+        for tt in range(tiles):
+            tsb[tt] = (tp[p, tt] + tr[tt].astype(jnp.float32)).astype(jnp.bfloat16)
+        tf[...] = tp[p, t] + tr[t].astype(jnp.float32)
+        elsewhere(lambda tt: sum_along(tt).start())
+    lax.fori_loop(early, heads, far_step, 0)
+    if fused:
+
+        def add_sum(tt):
+            arrival(tz.at[tt], zt_recv.at[tt])
+            tf[...] += tz[tt].astype(jnp.float32)
+
+        elsewhere(add_sum)
+        tfb[...] = tf[...].astype(jnp.bfloat16)
+        for k in range(3):
+            spread(k).start()
+        to[c, p] = tfb[...]
 
     k_out[:, group(c)] = dk[0, c]
     v_out[:, group(c)] = dk[1, c]
@@ -318,6 +470,26 @@
         def _():
             for cc in range(2):
                 stat_far(d, cc).wait_send()
+
+    if fused:
+        for cc, pp in ((o, p), (c, 1 - p), (o, 1 - p)):
+            arrival(to.at[cc, pp], fin_recv.at[cc, pp])
+        for hh in range(2):
+            for cc in range(2):
+                spot = pl.ds(hh * half_rows, half_rows), pl.ds(cc * cols, cols)
+                tk_out[spot] = to[cc, hh, 0]
+                tv_out[spot] = to[cc, hh, 1]
+        for k in range(3):
+            spread(k).wait_send()
+        sum_across.wait_send()
+
+        def end_text(tt):
+            for a in range(2):
+                text_gather(a, tt).wait_send()
+            text_across(tt).wait_send()
+            sum_along(tt).wait_send()
+
+        elsewhere(end_text)
 
     k_out[:, group(o)] = rk[0]
     v_out[:, group(o)] = rk[1]
@@ -366,17 +538,46 @@
         jnp.concatenate([stats, empty], axis=2),
         jnp.concatenate([empty, stats], axis=2),
     )
-    text_k = lax.all_gather(text_keys, "ta", axis=0, tiled=True)
-    text_v = lax.all_gather(text_values, "ta", axis=0, tiled=True)
-    text_count = text_k.shape[0]
+    text_rows = text_keys.shape[0]
+    text_count = tiles * text_rows
+    half_rows = text_rows // 2
+    fused = lax.axis_size("ha") == 4 and text_rows % 32 == 0
+    bf16, f32 = jnp.bfloat16, jnp.float32
+    dma = pltpu.SemaphoreType.DMA
+    if fused:
+        text_k, text_v = text_keys, text_values
+        text_out = jax.ShapeDtypeStruct((text_rows, hidden), bf16)
+        text_scratch = [
+            pltpu.VMEM((tiles, 2, 2, half_rows, cols), bf16),
+            pltpu.VMEM((2, tiles, 2, half_rows, cols), f32),
+            pltpu.VMEM((2, tiles, 2, half_rows, cols), bf16),
+            pltpu.VMEM((tiles, 2, half_rows, cols), bf16),
+            pltpu.VMEM((2, half_rows, cols), f32),
+            pltpu.VMEM((tiles, 2, half_rows, cols), bf16),
+            pltpu.VMEM((tiles, 2, half_rows, cols), bf16),
+            pltpu.VMEM((2, half_rows, cols), bf16),
+            pltpu.VMEM((2, 2, 2, half_rows, cols), bf16),
+            dma((2, tiles)),
+            dma((2, tiles)),
+            dma((tiles,)),
+            dma((tiles,)),
+            dma((2,)),
+            dma((tiles,)),
+            dma((tiles,)),
+            dma((3,)),
+            dma((2, 2)),
+        ]
+    else:
+        text_k = lax.all_gather(text_keys, "ta", axis=0, tiled=True)
+        text_v = lax.all_gather(text_values, "ta", axis=0, tiled=True)
+        text_out = jax.ShapeDtypeStruct((text_count, cols), f32)
+        text_scratch = []
     vmem = pl.BlockSpec(memory_space=pltpu.VMEM)
     smem = pl.BlockSpec(memory_space=pltpu.SMEM)
-    bf16, f32 = jnp.bfloat16, jnp.float32
-    dma = pltpu.SemaphoreType.DMA
     query_grad, key_grad, value_grad, key_text, value_text = pl.pallas_call(
-        functools.partial(kernel, tiles, heads, size),
+        functools.partial(kernel, tiles, heads, size, fused),
         out_shape=[jax.ShapeDtypeStruct((rows, hidden), bf16)] * 3
-        + [jax.ShapeDtypeStruct((text_count, cols), f32)] * 2,
+        + [text_out] * 2,
         in_specs=[vmem] * 7 + [smem] * 2,
         out_specs=[vmem] * 5,
         scratch_shapes=[
@@ -403,7 +604,9 @@
             dma((3, 2, heads)),
             dma((2, heads)),
             dma((2, heads)),
-        ],
+            pltpu.VMEM((2 * rows, cols), f32),
+        ]
+        + text_scratch,
         compiler_params=pltpu.CompilerParams(
             collective_id=0, has_side_effects=True, vmem_limit_bytes=48 * 1024 * 1024
         ),
@@ -422,6 +625,10 @@
         window_reach,
     )
 
+    grads = tuple(grad.reshape(shape) for grad in (query_grad, key_grad, value_grad))
+    if fused:
+        return grads + (key_text, value_text)
+
     def text_total(part):
         whole = jnp.zeros((2, text_count, cols), f32)
         whole = lax.dynamic_update_slice_in_dim(whole, part[None], half, 0)
@@ -429,13 +636,7 @@
         return lax.psum_scatter(whole, "ta", scatter_dimension=0, tiled=True)
 
     totals = lax.psum((text_total(key_text), text_total(value_text)), "ha")
-    return (
-        query_grad.reshape(shape),
-        key_grad.reshape(shape),
-        value_grad.reshape(shape),
-        totals[0].astype(bf16),
-        totals[1].astype(bf16),
-    )
+    return grads + (totals[0].astype(bf16), totals[1].astype(bf16))
 
 
 def solution(mesh):

time: 171 us -> 68.1 us (0.40)
  blocking collectives: 47.7 us -> 0 us
  waiting for transfers between devices: 41.9 us -> 0 us
  between operations: 14.8 us -> 1.39 us
  local copies, waits for them, and re-layouts: 21 us -> 10.4 us
  Pallas kernels: 44.4 us -> 54.1 us
    reduce_scatter x2 -> x0, waiting for transfers between devices: 41.9 us -> none  [text_total(): return lax.psum_scatter(whole, 'ta', scatter_dimension=0, tiled=True)]
    all_gather x2 -> x0, blocking collectives: 32 us -> none  [the longest x1 16.4 us: per_device(): text_k = lax.all_gather(text_keys, 'ta', axis=0, tiled=True)]
    psum x1 -> x0, blocking collectives: 15.6 us -> none  [per_device(): totals = lax.psum((text_total(key_text), text_total(value_text)), 'ha')]
    dynamic_update_slice x2 -> x0, local copies, waits for them, and re-layouts: 11.1 us -> none  [text_total(): whole = lax.dynamic_update_slice_in_dim(whole, part[None], half, 0)]
    pallas_call x1, Pallas kernels: 44.4 us -> 54.1 us  [per_device(): pl.pallas_call(functools.partial(kernel, tiles, heads, size, fused), out_...]
    unnamed x22 -> x18, local copies, waits for them, and re-layouts: 8.46 us -> 9.38 us
  transfers between devices with their start and end apart: 2 -> 0, of which waited for: 2 -> 0; matrix products, arithmetic and copies ran while one was open for 4% -> 0% of each run, Pallas kernels for 0% -> 0%
where the time goes in v2:
time: 68.1 us; the launch traced here: 67 us
  Pallas kernels  54.1 us (79%)
  local copies, waits for them, and re-layouts  10.4 us (15%)
  between operations  1.39 us (2%)
  other arithmetic  1.01 us (1%)
    pallas_call x1, Pallas kernels, per_device(): pl.pallas_call(functools.partial(kernel, tiles, heads, size, fused), out_...  54.1 us
    unnamed x18, local copies, waits for them, and re-layouts  9.38 us

profile of v2, /device:TPU:0, one launch (start us, length us, event | category | flops | bytes accessed | tf_op | source)
XLA Modules:
  0.0 67.0 jit_solution(11314362189660783605)
XLA Ops:
  0.6 0.0 copy-start
  1.4 0.8 %copy.20.reach = s32[12,2]{1,0:T(8,128)S(1)} copy(s32[12,2]{0,1:T(2,128)} %param.19) | data formatting | bytes 192 | tf_op args[9]
  2.1 1.0 %copy.19 = f32[192,12]{0,1:T(8,128)S(1)} copy(f32[192,12]{1,0:T(8,128)} %bitcast.19) | data formatting | bytes 18432 | tf_op jit(solution)/shard_map/reshape | solution.py:531
  3.1 0.9 %broadcast_multiply_fusion = f32[6,4,8,12]{3,2,1,0:T(8,128)S(1)} fusion(f32[6,4,8,12]{3,2,1,0:T(8,128)} %param.14), kind=kLoop, calls=%fused_computation.1 | loop fusion | flops 2304 | bytes 18432 | tf_op jit(solution)/shard_map/mul | solution.py:534
  4.0 0.1 copy.18
  4.1 0.0 copy-start.4
  4.1 0.1 pad_select_fusion.stat_in
  4.2 0.0 copy-done
  4.2 0.8 %copy-done.4 = bf16[32,1536]{1,0:T(8,128)(2,1)S(1)} copy-done((bf16[32,1536]{1,0:T(8,128)(2,1)S(1)}, bf16[32,1536]{1,0:T(8,128)(2,1)}, u32[]{:S(2)}) %copy-start.4) | copy-done | bytes 98328
  5.0 0.0 copy-start.1
  5.0 1.1 %copy-done.1 = bf16[6,4,8,1536]{3,2,1,0:T(8,128)(2,1)S(1)} copy-done((bf16[6,4,8,1536]{3,2,1,0:T(8,128)(2,1)S(1)}, bf16[6,4,8,1536]{3,2,1,0:T(8,128)(2,1)}, u32[]{:S(2)}) %copy-start.1) | copy-done | bytes 589848
  6.1 0.0 copy-start.2
  6.1 1.1 %copy-done.2 = bf16[6,4,8,1536]{3,2,1,0:T(8,128)(2,1)S(1)} copy-done((bf16[6,4,8,1536]{3,2,1,0:T(8,128)(2,1)S(1)}, bf16[6,4,8,1536]{3,2,1,0:T(8,128)(2,1)}, u32[]{:S(2)}) %copy-start.2) | copy-done | bytes 589848
  7.1 0.0 copy-start.3
  7.1 1.1 %copy-done.3 = bf16[6,4,8,1536]{3,2,1,0:T(8,128)(2,1)S(1)} copy-done((bf16[6,4,8,1536]{3,2,1,0:T(8,128)(2,1)S(1)}, bf16[6,4,8,1536]{3,2,1,0:T(8,128)(2,1)}, u32[]{:S(2)}) %copy-start.3) | copy-done | bytes 589848
  8.2 0.0 copy-start.5
  8.2 0.9 %copy-done.5 = bf16[32,1536]{1,0:T(8,128)(2,1)S(1)} copy-done((bf16[32,1536]{1,0:T(8,128)(2,1)S(1)}, bf16[32,1536]{1,0:T(8,128)(2,1)}, u32[]{:S(2)}) %copy-start.5) | copy-done | bytes 98328
  9.1 54.1 %shard_map.137 = (bf16[192,1536]{1,0:T(8,128)(2,1)S(1)}, bf16[192,1536]{1,0:T(8,128)(2,1)S(1)}, bf16[192,1536]{1,0:T(8,128)(2,1)S(1)}, bf16[32,1536]{1,0:T(8,128)(2,1)S(1)}, bf16[32,1536]{1,0:T(8,128)(2,1)S(1)}) custom-call(bf16[192,1536]{1,0:T(8,128)(2,1)S(1)} %bitcast.14, bf16[192,1536]{1,0:T(8,128)(2,1)S(1)} %bitcast.15, bf16[192,1536]{1,0:T(8,128)(2,1)S(1)} %bitcast.16, ...), custom_call_target="tpu_custom_call" | custom-call | flops 7927234560 | bytes 4718592 | tf_op jit(solution)/shard_map/pallas_call | solution.py:577
  63.2 0.8 %copy.27 = bf16[6,4,8,1536]{3,2,1,0:T(8,128)(2,1)} copy(bf16[6,4,8,1536]{3,2,1,0:T(8,128)(2,1)S(1)} %bitcast.13) | data formatting | bytes 1179648
  64.0 0.8 %copy.28 = bf16[6,4,8,1536]{3,2,1,0:T(8,128)(2,1)} copy(bf16[6,4,8,1536]{3,2,1,0:T(8,128)(2,1)S(1)} %bitcast.12) | data formatting | bytes 1179648
  64.9 0.8 %copy.29 = bf16[6,4,8,1536]{3,2,1,0:T(8,128)(2,1)} copy(bf16[6,4,8,1536]{3,2,1,0:T(8,128)(2,1)S(1)} %bitcast.11) | data formatting | bytes 1179648
  65.7 0.6 copy.30
  66.3 0.6 copy.31
  (3 shorter events, 0.0 us)
Async XLA Ops:
  0.6 3.6 %copy-start = (bf16[6,4,8,1536]{3,2,1,0:T(8,128)(2,1)S(1)}, bf16[6,4,8,1536]{3,2,1,0:T(8,128)(2,1)}, u32[]{:S(2)}) copy-start(bf16[6,4,8,1536]{3,2,1,0:T(8,128)(2,1)} %param.10) | copy-start | bytes 1769476
  4.1 0.9 %copy-start.4 = (bf16[32,1536]{1,0:T(8,128)(2,1)S(1)}, bf16[32,1536]{1,0:T(8,128)(2,1)}, u32[]{:S(2)}) copy-start(bf16[32,1536]{1,0:T(8,128)(2,1)} %text_k.1) | copy-start | bytes 294916
  5.0 1.1 %copy-start.1 = (bf16[6,4,8,1536]{3,2,1,0:T(8,128)(2,1)S(1)}, bf16[6,4,8,1536]{3,2,1,0:T(8,128)(2,1)}, u32[]{:S(2)}) copy-start(bf16[6,4,8,1536]{3,2,1,0:T(8,128)(2,1)} %param.13) | copy-start | bytes 1769476
  6.1 1.1 %copy-start.2 = (bf16[6,4,8,1536]{3,2,1,0:T(8,128)(2,1)S(1)}, bf16[6,4,8,1536]{3,2,1,0:T(8,128)(2,1)}, u32[]{:S(2)}) copy-start(bf16[6,4,8,1536]{3,2,1,0:T(8,128)(2,1)} %param.11) | copy-start | bytes 1769476
  7.1 1.1 %copy-start.3 = (bf16[6,4,8,1536]{3,2,1,0:T(8,128)(2,1)S(1)}, bf16[6,4,8,1536]{3,2,1,0:T(8,128)(2,1)}, u32[]{:S(2)}) copy-start(bf16[6,4,8,1536]{3,2,1,0:T(8,128)(2,1)} %param.12) | copy-start | bytes 1769476
  8.2 0.9 %copy-start.5 = (bf16[32,1536]{1,0:T(8,128)(2,1)S(1)}, bf16[32,1536]{1,0:T(8,128)(2,1)}, u32[]{:S(2)}) copy-start(bf16[32,1536]{1,0:T(8,128)(2,1)} %text_v.1) | copy-start | bytes 294916

commit v3 on v2

--- a/solution.py
+++ b/solution.py
@@ -62,6 +62,8 @@
     kv_send,
     kv_recv,
     aq,
+    qs,
+    out_sem,
     *text_scratch,
 ):
     rows = q_in.shape[0]
@@ -101,8 +103,9 @@
     if fused:
         (tw, tp, tb, tr, tf, tsb, tz, tfb, to) = text_scratch[:9]
         (tg_send, tg_recv, tx_send, tx_recv, xr_sem, zt_send, zt_recv, fin_send, fin_recv) = (
-            text_scratch[9:]
-        )
+            text_scratch[9:18]
+        )
+        tl_sem = text_scratch[18]
         half_rows = tw.shape[3]
         p = lax.div(ha, 2)
         across = (grp, t, lax.rem(ha + 2, 4))
@@ -141,6 +144,13 @@
                 device_id_type=MESH_ID,
             )
 
+        def text_own(a, hh):
+            return pltpu.make_async_copy(
+                (text_k, text_v)[a].at[pl.ds(hh * half_rows, half_rows), group(c)],
+                tw.at[t, hh, a],
+                tl_sem.at[a, hh],
+            )
+
         def text_across(tt):
             return pltpu.make_async_remote_copy(
                 src_ref=tw.at[tt, p],
@@ -243,6 +253,9 @@
                 text_gather(a, tt).start()
 
         elsewhere(send_text)
+        for a in range(2):
+            for hh in range(2):
+                text_own(a, hh).start()
     for a in range(4):
         pair(a).start()
         own(a).start()
@@ -273,10 +286,6 @@
             rq[1 + d] = jnp.zeros_like(rq[1 + d])
 
     if fused:
-        for hh in range(2):
-            for a in range(2):
-                tw[t, hh, a] = (text_k, text_v)[a][hh * half_rows : (hh + 1) * half_rows, group(c)]
-
         def forward_text(tt):
             for a in range(2):
                 arrival(tw.at[tt, p, a], tg_recv.at[a, tt])
@@ -288,7 +297,11 @@
         own(a).wait()
         pair(a).wait_recv()
     stat_pair.wait_recv()
-    st[0] = stat_in[c] + sw[0, o]
+    def fill(s, values):
+        st[s, 0:8] = values[0:8] * LOG2E
+        st[s, 8:16] = values[8:16]
+
+    fill(0, stat_in[c] + sw[0, o])
 
     def term(s, b, j):
         target = partner if s == 0 else (grp, near[s - 1], base + b)
@@ -370,6 +383,9 @@
     lax.fori_loop(0, heads, near_step, 0)
     if fused:
         elsewhere(lambda tt: arrival(tw.at[tt, 1 - p], tx_recv.at[tt]))
+        for a in range(2):
+            for hh in range(2):
+                text_own(a, hh).wait()
     lax.fori_loop(0, heads, text_step, 0)
     if fused:
         sum_across.start()
@@ -381,7 +397,7 @@
             for b in range(2):
                 dst = sw.at[1 + d, b]
                 pltpu.make_async_copy(dst, dst, stat_recv.at[1 + d, b]).wait()
-            st[1 + d] = sw[1 + d, 0] + sw[1 + d, 1]
+            fill(1 + d, sw[1 + d, 0] + sw[1 + d, 1])
 
     def far_step(j, carry):
         for d in range(2):
@@ -391,7 +407,7 @@
                 for a in range(2):
                     for b in range(2):
                         far_wait(d, b, a, j)
-                seen = reach[c * heads + j, 1 - d] >= 1
+                seen = reach[1 - d, c * heads + j] >= 1
                 lse = st[1 + d, pl.ds(j, 1), :] + jnp.where(seen, 0.0, HIDDEN_LSE)
                 out_dot = st[1 + d, pl.ds(8 + j, 1), :]
                 dq_far, dk_far, dv_far = grads(
@@ -440,27 +456,22 @@
             spread(k).start()
         to[c, p] = tfb[...]
 
-    k_out[:, group(c)] = dk[0, c]
-    v_out[:, group(c)] = dk[1, c]
-
-    def finish(j, carry):
+    def put(a, index, source):
+        return pltpu.make_async_copy(
+            source, (k_out, v_out)[a].at[:, group(index)], out_sem.at[a, index]
+        )
+
+    for a in range(2):
+        put(a, c, dk.at[a, c]).start()
+
+    def finish_kv(j, carry):
         for a in range(2):
             kv(a, j).wait()
-        term(0, o, j).wait_send()
-        term_wait(0, o, j)
-        for d in range(2):
-
-            @pl.when(has[d])
-            def _():
-                for b in range(2):
-                    term_wait(1 + d, b, j)
-                    term(1 + d, b, j).wait_send()
-                    for a in range(2):
-                        far(d, b, a, j).wait_send()
-
         return carry
 
-    lax.fori_loop(0, heads, finish, 0)
+    lax.fori_loop(0, heads, finish_kv, 0)
+    for a in range(2):
+        put(a, o, rk.at[a]).start()
     stat_pair.wait_send()
     for a in range(4):
         pair(a).wait_send()
@@ -491,18 +502,56 @@
 
         elsewhere(end_text)
 
-    k_out[:, group(o)] = rk[0]
-    v_out[:, group(o)] = rk[1]
-
-    def total(own_part, index):
+    def total(own_part, index, j):
         return (
             own_part.astype(jnp.float32)
-            + rq[1, index].astype(jnp.float32)
-            + rq[2, index].astype(jnp.float32)
-        ).astype(q_out.dtype)
-
-    q_out[:, group(c)] = total(dq[0, c], c)
-    q_out[:, group(o)] = total(rq[0, o], o)
+            + rq[1, index, :, head(j)].astype(jnp.float32)
+            + rq[2, index, :, head(j)].astype(jnp.float32)
+        ).astype(jnp.bfloat16)
+
+    def put_query(index, j):
+        return pltpu.make_async_copy(
+            qs.at[index, :, head(j)],
+            q_out.at[:, group_head(index, j)],
+            out_sem.at[2 + index, j],
+        )
+
+    def finish(j, carry):
+        term(0, o, j).wait_send()
+        term_wait(0, o, j)
+        for d in range(2):
+
+            @pl.when(has[d])
+            def _():
+                for b in range(2):
+                    for a in range(2):
+                        far(d, b, a, j).wait_send()
+                    term_wait(1 + d, b, j)
+
+        qs[c, :, head(j)] = total(dq[0, c, :, head(j)], c, j)
+        qs[o, :, head(j)] = total(rq[0, o, :, head(j)], o, j)
+        for index in range(2):
+            put_query(index, j).start()
+        return carry
+
+    lax.fori_loop(0, heads, finish, 0)
+
+    def finish_send(j, carry):
+        for d in range(2):
+
+            @pl.when(has[d])
+            def _():
+                for b in range(2):
+                    term(1 + d, b, j).wait_send()
+
+        for index in range(2):
+            put_query(index, j).wait()
+        return carry
+
+    lax.fori_loop(0, heads, finish_send, 0)
+    for a in range(2):
+        put(a, c, dk.at[a, c]).wait()
+        put(a, o, rk.at[a]).wait()
 
 
 def per_device(
@@ -531,7 +580,7 @@
         turned = values.reshape(rows, head_count).T.reshape(2, heads, rows)
         return jnp.pad(turned, ((0, 0), (0, 8 - heads), (0, 0)))
 
-    stats = jnp.concatenate([stat(logsumexp * LOG2E), stat(out_dot)], axis=1)
+    stats = jnp.concatenate([stat(logsumexp), stat(out_dot)], axis=1)
     empty = jnp.zeros_like(stats)
     stats = jnp.where(
         half == 0,
@@ -566,6 +615,7 @@
             dma((tiles,)),
             dma((3,)),
             dma((2, 2)),
+            dma((2, 2)),
         ]
     else:
         text_k = lax.all_gather(text_keys, "ta", axis=0, tiled=True)
@@ -574,12 +624,13 @@
         text_scratch = []
     vmem = pl.BlockSpec(memory_space=pltpu.VMEM)
     smem = pl.BlockSpec(memory_space=pltpu.SMEM)
+    hbm = pl.BlockSpec(memory_space=pltpu.HBM)
     query_grad, key_grad, value_grad, key_text, value_text = pl.pallas_call(
         functools.partial(kernel, tiles, heads, size, fused),
         out_shape=[jax.ShapeDtypeStruct((rows, hidden), bf16)] * 3
         + [text_out] * 2,
-        in_specs=[vmem] * 7 + [smem] * 2,
-        out_specs=[vmem] * 5,
+        in_specs=[hbm] * 4 + [vmem] + [hbm if fused else vmem] * 2 + [smem] * 2,
+        out_specs=[hbm] * 3 + [vmem] * 2,
         scratch_shapes=[
             pltpu.VMEM((3, 2, rows, cols), bf16),
             pltpu.VMEM((3, 2, rows, cols), bf16),
@@ -605,10 +656,12 @@
             dma((2, heads)),
             dma((2, heads)),
             pltpu.VMEM((2 * rows, cols), f32),
+            pltpu.VMEM((2, rows, cols), bf16),
+            dma((4, heads)),
         ]
         + text_scratch,
         compiler_params=pltpu.CompilerParams(
-            collective_id=0, has_side_effects=True, vmem_limit_bytes=48 * 1024 * 1024
+            collective_id=0, has_side_effects=True, vmem_limit_bytes=62 * 1024 * 1024
         ),
         cost_estimate=pl.CostEstimate(
             flops=20 * rows * rows * 7 * hidden, bytes_accessed=16 * rows * hidden, transcendentals=0
@@ -622,7 +675,7 @@
         text_k,
         text_v,
         text_length,
-        window_reach,
+        window_reach.T,
     )
 
     grads = tuple(grad.reshape(shape) for grad in (query_grad, key_grad, value_grad))

time: 68.1 us -> 65.9 us (0.968)
  local copies, waits for them, and re-layouts: 10.4 us -> 6.86 us
  Pallas kernels: 54.1 us -> 55.8 us
    unnamed x18 -> x15, local copies, waits for them, and re-layouts: 9.38 us -> 5.79 us
    pallas_call x1, Pallas kernels: 54.1 us -> 55.8 us  [per_device(): pl.pallas_call(functools.partial(kernel, tiles, heads, size, fused), out_...]
    mul x1 -> x0, other arithmetic: 0.92 us -> none  [per_device(): stats = jnp.concatenate([stat(logsumexp * LOG2E), stat(out_dot)], axis=1)]
where the time goes in v3:
time: 65.9 us; the launch traced here: 64.8 us
  Pallas kernels  55.8 us (85%)
  local copies, waits for them, and re-layouts  6.86 us (10%)
  between operations  1.37 us (2%)
  other arithmetic  0.71 us (1%)
    pallas_call x1, Pallas kernels, per_device(): pl.pallas_call(functools.partial(kernel, tiles, heads, size, fused), out_...  55.8 us
    unnamed x15, local copies, waits for them, and re-layouts  5.79 us

profile of v3, /device:TPU:0, one launch (start us, length us, event | category | flops | bytes accessed | tf_op | source)
XLA Modules:
  0.0 64.8 jit_solution(14398340767439695374)
XLA Ops:
  0.6 0.0 copy-start.2
  1.3 1.0 %copy.17 = f32[192,12]{0,1:T(8,128)S(1)} copy(f32[192,12]{1,0:T(8,128)} %bitcast.15) | data formatting | bytes 18432 | tf_op jit(solution)/shard_map/reshape | solution.py:580
  2.3 0.0 copy-done.2
  2.3 0.1 copy.18
  2.4 0.7 %pad_select_fusion.stat_in = f32[2,16,384]{2,1,0:T(8,128)} fusion(f32[2,16,192]{2,1,0:T(8,128)S(1)} %select_maximum_fusion, pred[]{:T(512)S(6)} %eq.5), kind=kLoop, calls=%fused_computation | loop fusion | flops 12288 | bytes 73729 | tf_op jit(solution)/shard_map/jit(_where)/select_n | solution.py:585
  3.1 55.8 %shard_map.137 = (bf16[192,1536]{1,0:T(8,128)(2,1)}, bf16[192,1536]{1,0:T(8,128)(2,1)}, bf16[192,1536]{1,0:T(8,128)(2,1)}, bf16[32,1536]{1,0:T(8,128)(2,1)}, bf16[32,1536]{1,0:T(8,128)(2,1)}) custom-call(bf16[192,1536]{1,0:T(8,128)(2,1)} %bitcast.19, bf16[192,1536]{1,0:T(8,128)(2,1)} %bitcast.20, bf16[192,1536]{1,0:T(8,128)(2,1)} %bitcast.21, ...), custom_call_target="tpu_custom_call" | custom-call | flops 7927234560 | bytes 4718592 | tf_op jit(solution)/shard_map/pallas_call | solution.py:628
  59.0 0.0 copy-start.1
  59.0 2.0 %copy.25 = bf16[6,4,8,1536]{3,2,1,0:T(8,128)(2,1)} copy(bf16[6,4,8,1536]{3,2,1,0:T(8,128)(2,1)} %bitcast.14) | data formatting | bytes 1179648
  61.0 0.0 copy-done.1
  61.0 0.0 copy-start
  61.0 0.8 %copy.26 = bf16[6,4,8,1536]{3,2,1,0:T(8,128)(2,1)} copy(bf16[6,4,8,1536]{3,2,1,0:T(8,128)(2,1)S(1)} %bitcast.13) | data formatting | bytes 1179648
  61.8 0.5 copy-done
  62.2 0.0 copy-start.4
  62.2 0.8 %copy.27 = bf16[6,4,8,1536]{3,2,1,0:T(8,128)(2,1)} copy(bf16[6,4,8,1536]{3,2,1,0:T(8,128)(2,1)S(1)} %bitcast.12) | data formatting | bytes 1179648
  63.1 0.1 copy-done.4
  63.2 0.0 copy-start.3
  63.2 0.6 copy.28
  63.9 0.3 copy-done.3
  64.1 0.6 copy.29
  (3 shorter events, 0.0 us)
Async XLA Ops:
  0.6 1.7 %copy-start.2 = (f32[6,4,8,12]{3,2,1,0:T(8,128)S(1)}, f32[6,4,8,12]{3,2,1,0:T(8,128)}, u32[]{:S(2)}) copy-start(f32[6,4,8,12]{3,2,1,0:T(8,128)} %param.15) | copy-start | bytes 27652
  59.0 2.0 %copy-start.1 = (bf16[192,1536]{1,0:T(8,128)(2,1)S(1)}, bf16[192,1536]{1,0:T(8,128)(2,1)}, u32[]{:S(2)}) copy-start(bf16[192,1536]{1,0:T(8,128)(2,1)} %get-tuple-element.11) | copy-start | bytes 1769476
  61.0 1.3 %copy-start = (bf16[192,1536]{1,0:T(8,128)(2,1)S(1)}, bf16[192,1536]{1,0:T(8,128)(2,1)}, u32[]{:S(2)}) copy-start(bf16[192,1536]{1,0:T(8,128)(2,1)} %get-tuple-element.12) | copy-start | bytes 1769476
  62.2 1.0 %copy-start.4 = (bf16[32,1536]{1,0:T(8,128)(2,1)S(1)}, bf16[32,1536]{1,0:T(8,128)(2,1)}, u32[]{:S(2)}) copy-start(bf16[32,1536]{1,0:T(8,128)(2,1)} %get-tuple-element.23) | copy-start | bytes 294916
  63.2 0.9 %copy-start.3 = (bf16[32,1536]{1,0:T(8,128)(2,1)S(1)}, bf16[32,1536]{1,0:T(8,128)(2,1)}, u32[]{:S(2)}) copy-start(bf16[32,1536]{1,0:T(8,128)(2,1)} %get-tuple-element.24) | copy-start | bytes 294916

commit v4 on v3

--- a/solution.py
+++ b/solution.py
@@ -630,7 +630,7 @@
         out_shape=[jax.ShapeDtypeStruct((rows, hidden), bf16)] * 3
         + [text_out] * 2,
         in_specs=[hbm] * 4 + [vmem] + [hbm if fused else vmem] * 2 + [smem] * 2,
-        out_specs=[hbm] * 3 + [vmem] * 2,
+        out_specs=[vmem] * 5,
         scratch_shapes=[
             pltpu.VMEM((3, 2, rows, cols), bf16),
             pltpu.VMEM((3, 2, rows, cols), bf16),
@@ -661,7 +661,7 @@
         ]
         + text_scratch,
         compiler_params=pltpu.CompilerParams(
-            collective_id=0, has_side_effects=True, vmem_limit_bytes=62 * 1024 * 1024
+            collective_id=0, has_side_effects=True, vmem_limit_bytes=412 * 128 * 1024
         ),
         cost_estimate=pl.CostEstimate(
             flops=20 * rows * rows * 7 * hidden, bytes_accessed=16 * rows * hidden, transcendentals=0

time: 65.9 us -> 62.1 us (0.942)
  Pallas kernels: 55.8 us -> 54.1 us
  local copies, waits for them, and re-layouts: 6.86 us -> 5.6 us
    pallas_call x1, Pallas kernels: 55.8 us -> 54.1 us  [per_device(): pl.pallas_call(functools.partial(kernel, tiles, heads, size, fused), out_...]
    unnamed x15 -> x13, local copies, waits for them, and re-layouts: 5.79 us -> 4.54 us
where the time goes in v4:
time: 62.1 us; the launch traced here: 61.2 us
  Pallas kernels  54.1 us (87%)
  local copies, waits for them, and re-layouts  5.6 us (9%)
  between operations  1.38 us (2%)
    pallas_call x1, Pallas kernels, per_device(): pl.pallas_call(functools.partial(kernel, tiles, heads, size, fused), out_...  54.1 us
    unnamed x13, local copies, waits for them, and re-layouts  4.54 us

profile of v4, /device:TPU:0, one launch (start us, length us, event | category | flops | bytes accessed | tf_op | source)
XLA Modules:
  0.0 61.2 jit_solution(3353629487735094368)
XLA Ops:
  0.6 0.0 copy-start.3
  1.3 1.0 %copy.17 = f32[192,12]{0,1:T(8,128)S(1)} copy(f32[192,12]{1,0:T(8,128)} %bitcast.16) | data formatting | bytes 18432 | tf_op jit(solution)/shard_map/reshape | solution.py:580
  2.3 0.0 copy-done.3
  2.3 0.0 copy-start.1
  2.3 0.1 copy.18
  2.4 0.0 copy-start
  2.4 0.0 copy-start.2
  2.4 0.1 pad_select_fusion.stat_in
  2.5 0.7 %copy-done.1 = bf16[32,1536]{1,0:T(8,128)(2,1)S(1)} copy-done((bf16[32,1536]{1,0:T(8,128)(2,1)S(1)}, bf16[32,1536]{1,0:T(8,128)(2,1)}, u32[]{:S(2)}) %copy-start.1) | copy-done | bytes 98328
  3.2 0.1 copy-done
  3.3 0.0 copy-done.2
  3.3 54.1 %shard_map.137 = (bf16[192,1536]{1,0:T(8,128)(2,1)S(1)}, bf16[192,1536]{1,0:T(8,128)(2,1)S(1)}, bf16[192,1536]{1,0:T(8,128)(2,1)S(1)}, bf16[32,1536]{1,0:T(8,128)(2,1)S(1)}, bf16[32,1536]{1,0:T(8,128)(2,1)S(1)}) custom-call(bf16[192,1536]{1,0:T(8,128)(2,1)} %bitcast.20, bf16[192,1536]{1,0:T(8,128)(2,1)} %bitcast.21, bf16[192,1536]{1,0:T(8,128)(2,1)} %bitcast.22, ...), custom_call_target="tpu_custom_call" | custom-call | flops 7927234560 | bytes 4718592 | tf_op jit(solution)/shard_map/pallas_call | solution.py:628
  57.4 0.8 %copy.25 = bf16[6,4,8,1536]{3,2,1,0:T(8,128)(2,1)} copy(bf16[6,4,8,1536]{3,2,1,0:T(8,128)(2,1)S(1)} %bitcast.14) | data formatting | bytes 1179648
  58.3 0.8 %copy.26 = bf16[6,4,8,1536]{3,2,1,0:T(8,128)(2,1)} copy(bf16[6,4,8,1536]{3,2,1,0:T(8,128)(2,1)S(1)} %bitcast.13) | data formatting | bytes 1179648
  59.1 0.8 %copy.27 = bf16[6,4,8,1536]{3,2,1,0:T(8,128)(2,1)} copy(bf16[6,4,8,1536]{3,2,1,0:T(8,128)(2,1)S(1)} %bitcast.12) | data formatting | bytes 1179648
  59.9 0.6 %copy.28 = bf16[32,1536]{1,0:T(8,128)(2,1)} copy(bf16[32,1536]{1,0:T(8,128)(2,1)S(1)} %get-tuple-element.23) | data formatting | bytes 196608
  60.5 0.6 %copy.29 = bf16[32,1536]{1,0:T(8,128)(2,1)} copy(bf16[32,1536]{1,0:T(8,128)(2,1)S(1)} %get-tuple-element.24) | data formatting | bytes 196608
  (3 shorter events, 0.0 us)
Async XLA Ops:
  0.6 1.7 %copy-start.3 = (f32[6,4,8,12]{3,2,1,0:T(8,128)S(1)}, f32[6,4,8,12]{3,2,1,0:T(8,128)}, u32[]{:S(2)}) copy-start(f32[6,4,8,12]{3,2,1,0:T(8,128)} %param.15) | copy-start | bytes 27652
  2.3 0.9 %copy-start.1 = (bf16[32,1536]{1,0:T(8,128)(2,1)S(1)}, bf16[32,1536]{1,0:T(8,128)(2,1)}, u32[]{:S(2)}) copy-start(bf16[32,1536]{1,0:T(8,128)(2,1)} %text_v.1) | copy-start | bytes 294916
  2.4 0.9 %copy-start = (bf16[32,1536]{1,0:T(8,128)(2,1)S(1)}, bf16[32,1536]{1,0:T(8,128)(2,1)}, u32[]{:S(2)}) copy-start(bf16[32,1536]{1,0:T(8,128)(2,1)} %text_k.1) | copy-start | bytes 294916
  2.4 0.9 %copy-start.2 = (s32[12,2]{0,1:T(2,128)S(1)}, s32[12,2]{0,1:T(2,128)}, u32[]{:S(2)}) copy-start(s32[12,2]{0,1:T(2,128)} %param.19) | copy-start | bytes 292
